TPU v7x, 1024 devices: a whole 8x8x8 slice. The times are simulated.
1024 devices in a mesh: expert: 64 (over x, y), head: 16 (over z, core).
Axes of the slice: x: 8, y: 8, z: 8, core: 2. Of those that a mesh axis runs over, the one named last changes fastest.
Arguments:
- latent: bfloat16 [2048, 1024], P('expert'), may hold values from -6 to 6
- routes: int32 [2048, 22], P('expert'), may hold values from 0 to 255, all different within a row; in each aligned block of 32 rows (0 to 31, 32 to 63, ...) at most 4 rows name the same one
- gate_q: int32 [2048, 22], P('expert'), may hold values from 1 to 255
- up_weight: bfloat16 [256, 1024, 2048], P('expert', None, 'head'), may hold values from -0.1875 to 0.1875
- down_weight: bfloat16 [256, 2048, 1024], P('expert', 'head'), may hold values from -0.125 to 0.125
- out_weight: bfloat16 [1024, 4096], P(None, 'head'), may hold values from -0.1875 to 0.1875
- cotangent: bfloat16 [2048, 4096], P('expert', 'head'), may hold values from -6 to 6
Outputs:
- mixed: bfloat16 [2048, 4096], P('expert', 'head')
- grad_up: bfloat16 [256, 1024, 2048], P('expert', None, 'head')
Inputs may be any that keep to these rules, and one draw needn't show every extreme that they name: `routes`: each row names 22 different experts. In each aligned block of 32 rows (the tokens of one index of expert) no expert is named by more than 4 rows, a bound that some block reaches.
All inputs are finite; a program needn't handle non-finite values.
Results may differ from a plain program's by a relative error of at most 0.029.
Values may be sent and summed in bfloat16 or wider, within the bound.
No kernel may reach another device: no remote copies, remote signals or barrier semaphores. Data moves between devices by JAX's collectives and lax.ppermute only.
A program may use at most 64 MiB of HBM per device.

v0:
```python
import jax
import jax.numpy as jnp
from jax import lax
from jax.experimental import pallas as pl
from jax.experimental.pallas import tpu as pltpu
from jax.sharding import Mesh, PartitionSpec as P

F32 = jnp.float32
BF16 = jnp.bfloat16
HEAD = ("z", "core")
QUAD = 4
CHUNKS = 4
BACK_VMEM, SEND_VMEM, FORWARD_VMEM, WEIGHT_VMEM = 53, 53, 50, 50
MIB = 2**20
MOST = 4
ROWS = 2 * MOST
ANY = pl.BlockSpec(memory_space=pl.ANY)
VMEM = pl.BlockSpec(memory_space=pltpu.VMEM)
SMEM = pl.BlockSpec(memory_space=pltpu.SMEM)


def call(kernel, outs, *args, scalars=0, flops=0, in_hbm=(), out_hbm=(), scratch=(), vmem=32):
    single = not isinstance(outs, (list, tuple))
    moved = sum(a.size * a.dtype.itemsize for a in args)
    ins = [SMEM if i < scalars else ANY if i in in_hbm else VMEM for i in range(len(args))]
    places = [ANY if i in out_hbm else VMEM for i in range(1 if single else len(outs))]
    return pl.pallas_call(
        kernel,
        out_shape=outs,
        in_specs=ins,
        out_specs=places[0] if single else places,
        scratch_shapes=scratch,
        compiler_params=pltpu.CompilerParams(vmem_limit_bytes=vmem * MIB),
        cost_estimate=pl.CostEstimate(flops=flops, bytes_accessed=2 * moved, transcendentals=0),
    )(*args)


def shape(*dims, dtype=BF16):
    return jax.ShapeDtypeStruct(dims, dtype)


def dot(a, b, dims, precision=None):
    return lax.dot_general(a, b, (dims, ((), ())), precision=precision, preferred_element_type=F32)


def halves(me_ref, rows):
    half = rows.shape[1] // 2
    first = me_ref[0] % 2 == 0
    left, right = rows[:, :half], rows[:, half:]
    return jnp.where(first, left, right), jnp.where(first, right, left)


def joined(me_ref, own, other):
    first = me_ref[0] % 2 == 0
    own, other = own.astype(F32), other.astype(F32)
    return jnp.concatenate([jnp.where(first, own, other), jnp.where(first, other, own)], axis=1)


def back_kernel(me_ref, cot_hbm, out_w_hbm, keep_ref, give_ref, cot_ref, out_w_ref, sems):
    copies = [
        pltpu.make_async_copy(out_w_hbm, out_w_ref, sems.at[0]),
        pltpu.make_async_copy(cot_hbm, cot_ref, sems.at[1]),
    ]
    for copy in copies:
        copy.start()
    for copy in copies:
        copy.wait()
    part = dot(cot_ref[...], out_w_ref[...], ((1,), (1,)))
    keep, give = halves(me_ref, part)
    keep_ref[...] = keep
    give_ref[...] = give.astype(BF16)


def spread_kernel(keep_ref, got_ref, o_ref):
    rows = (keep_ref[...] + got_ref[...].astype(F32)).astype(BF16)
    for z in range(o_ref.shape[0]):
        o_ref[z] = rows


def sum_kernel(i_ref, o_ref):
    o_ref[...] = jnp.sum(i_ref[...].astype(F32), axis=0).astype(BF16)


def pick_kernel(me_ref, table_ref, coef_ref):
    count, tokens = coef_ref.shape
    top = table_ref.shape[0] // 2
    row = lax.broadcasted_iota(jnp.int32, (count, tokens), 0)
    expert = QUAD * (row // ROWS) + me_ref[0]
    score = jnp.zeros((count, tokens), jnp.int32)
    for k in range(top):
        q = table_ref[top + k : top + k + 1, :]
        score = score + jnp.where(table_ref[k : k + 1, :] == expert, q, 0)
    score = score.astype(F32)
    named = score > 0.0
    earlier = lax.broadcasted_iota(jnp.int32, (tokens, tokens), 0)
    later = lax.broadcasted_iota(jnp.int32, (tokens, tokens), 1)
    before = jnp.where(earlier < later, 1.0, 0.0).astype(BF16)
    rank = dot(jnp.where(named, 1.0, 0.0).astype(BF16), before, ((1,), (0,)))
    here = named & (rank == (row % MOST).astype(F32))
    coef_ref[...] = jnp.where(here, score, 0.0).astype(BF16)


def send_kernel(me_ref, table_ref, coef_ref, latent_ref, own_ref, other_ref, send_ref, buf, sems):
    count = send_ref.shape[0]
    top = table_ref.shape[0] // 2
    step = count // CHUNKS
    back = joined(me_ref, own_ref[...], other_ref[...]).astype(BF16)
    latent = latent_ref[...]
    total = jnp.sum(table_ref[top:, :].astype(F32), axis=0, keepdims=True)
    is_latent = lax.broadcasted_iota(jnp.int32, (step, 1), 0) % ROWS < MOST
    copies = []
    for i in range(CHUNKS):
        at = pl.ds(step * i, step)
        coef = coef_ref[at, :].astype(F32)
        gate = jnp.sum(coef / total, axis=1, keepdims=True)
        pick = jnp.where(coef > 0.0, 1.0, 0.0).astype(BF16)
        latent_rows = dot(pick, latent, ((1,), (0,)))
        back_rows = dot(pick, back, ((1,), (0,)))
        buf[at, :] = jnp.where(is_latent, latent_rows, gate * back_rows).astype(BF16)
        copies.append(pltpu.make_async_copy(buf.at[at, :], send_ref.at[at, :], sems.at[i]))
        copies[-1].start()
    for copy in copies:
        copy.wait()


def pack_kernel(me_ref, up_ref, down_ref, *outs):
    width, unit = up_ref.shape[1], up_ref.shape[2]
    for d, o_ref in enumerate(outs, 1):
        expert = me_ref[0] ^ d
        o_ref[0:width, :] = up_ref[expert]
        for b in range(width // unit):
            o_ref[width + unit * b : width + unit * (b + 1), :] = down_ref[
                expert, :, unit * b : unit * (b + 1)
            ]


class Copies:
    def __init__(self, sems):
        self.sems, self.used = sems, 0

    def start(self, source, target):
        copy = pltpu.make_async_copy(source, target, self.sems.at[self.used])
        self.used += 1
        copy.start()
        return copy

    def start_down(self, me, down_hbm, packs, down_ref):
        unit, width = down_hbm.shape[1:]
        started = [self.start(down_hbm.at[me], down_ref.at[0:unit, :])]
        for d, p in enumerate(packs, 1):
            at = pl.ds(unit * d, unit)
            for b in range(width // unit):
                block = p.at[pl.ds(width + unit * b, unit), :]
                started.append(self.start(block, down_ref.at[at, pl.ds(unit * b, unit)]))
        return started

    def start_up(self, me, up_hbm, packs, up_ref):
        width, unit = up_hbm.shape[1:]
        started = [self.start(up_hbm.at[me], up_ref.at[:, 0:unit])]
        for d, p in enumerate(packs, 1):
            started.append(self.start(p.at[pl.ds(0, width), :], up_ref.at[:, pl.ds(unit * d, unit)]))
        return started


def wait(copies):
    for copy in copies:
        copy.wait()


def latent_rows_of(count):
    return lax.broadcasted_iota(jnp.int32, (count, 1), 0) % ROWS < MOST


def forward_kernel(me_ref, rows_ref, up_hbm, down_hbm, *refs):
    packs, refs = refs[: QUAD - 1], refs[QUAD - 1 :]
    out_hbm, up_ref, down_ref, out_ref, sems = refs
    count, half = out_ref.shape
    copies = Copies(sems)
    ups = copies.start_up(me_ref[0], up_hbm, packs, up_ref)
    downs = copies.start_down(me_ref[0], down_hbm, packs, down_ref)
    is_latent = latent_rows_of(count)
    wait(ups)
    act = jnp.maximum(dot(rows_ref[...], up_ref[...], ((1,), (0,))), 0.0)
    hidden = act * act
    hidden = jnp.where(is_latent, hidden, pltpu.roll(hidden, MOST, 0)).astype(BF16)
    wait(downs)
    left = dot(hidden, down_ref[:, :half], ((1,), (0,)))
    right = dot(hidden, down_ref[:, half:], ((1,), (0,)))
    out_ref[...] = jnp.where(is_latent, left, right).astype(BF16)
    wait([copies.start(out_ref, out_hbm)])


def weight_kernel(me_ref, rows_ref, up_hbm, down_hbm, *refs):
    packs, refs = refs[: QUAD - 1], refs[QUAD - 1 :]
    outs_hbm, refs = refs[:QUAD], refs[QUAD:]
    up_ref, down_ref, grad_ref, sems = refs
    unit = up_hbm.shape[2]
    count = rows_ref.shape[0]
    copies = Copies(sems)
    ups = copies.start_up(me_ref[0], up_hbm, packs, up_ref)
    downs = copies.start_down(me_ref[0], down_hbm, packs, down_ref)
    wait(ups)
    rows = rows_ref[...]
    act = jnp.maximum(dot(rows, up_ref[...], ((1,), (0,))), 0.0)
    wait(downs)
    hidden_grad = pltpu.roll(dot(rows, down_ref[...], ((1,), (1,))), count - MOST, 0)
    pre_grad = jnp.where(latent_rows_of(count), hidden_grad * 2.0 * act, 0.0).astype(BF16)
    grad_ref[...] = dot(rows, pre_grad, ((0,), (0,))).astype(BF16)
    wait([copies.start(grad_ref.at[:, pl.ds(unit * d, unit)], o) for d, o in enumerate(outs_hbm)])


def combine_kernel(me_ref, rows_ref, coef_ref, gate_ref, keep_ref, give_ref):
    count = rows_ref.shape[0]
    is_left = lax.broadcasted_iota(jnp.int32, (count, 1), 0) % ROWS < MOST
    coef = coef_ref[...].astype(F32)
    left = jnp.where(is_left, coef, 0.0).astype(BF16)
    right = jnp.where(is_left, 0.0, coef).astype(BF16)
    rows = rows_ref[...]
    total = jnp.sum(gate_ref[...].astype(F32), axis=1, keepdims=True)
    parts = [dot(c, rows, ((0,), (0,))) / total for c in (left, right)]
    keep, give = halves(me_ref, jnp.concatenate(parts, axis=1))
    keep_ref[...] = keep
    give_ref[...] = give.astype(BF16)


def mixed_kernel(me_ref, own_ref, other_ref, out_w_ref, o_ref):
    combined = joined(me_ref, own_ref[...], other_ref[...]).astype(BF16)
    o_ref[...] = dot(combined, out_w_ref[...], ((1,), (0,))).astype(BF16)


def grad_kernel(me_ref, *refs):
    grads, o_ref = refs[:-1], refs[-1]
    for d, g_ref in enumerate(grads):
        o_ref[me_ref[0] ^ d] = g_ref[...]


def exchange(rows, axis):
    peers = lax.axis_size(axis)
    split = rows.reshape(peers, rows.shape[0] // peers, rows.shape[1])
    moved = lax.all_to_all(split, axis, split_axis=0, concat_axis=0, tiled=True)
    return moved.reshape(rows.shape)


def swap(array, distance, back=False):
    chips = lax.axis_size("z")
    pairs = []
    for z in range(chips):
        for core in range(2):
            to = (z + 2 * core - 1) % chips if distance > 1 else z
            pairs.append((2 * z + core, 2 * to + core ^ (distance % 2)))
    return lax.ppermute(array, HEAD, [(b, a) for a, b in pairs] if back else pairs)


def sum_over_head(keep, give, beside=()):
    chips = lax.axis_size("z")
    spread = call(spread_kernel, shape(chips, *keep.shape), keep, swap(give, 1))
    moved = lax.all_to_all(spread, "z", split_axis=0, concat_axis=0, tiled=True)
    moved, *beside = lax.optimization_barrier((moved, *beside))
    own = call(sum_kernel, shape(*keep.shape), moved)
    return own, swap(own, 1), *beside


def per_device(latent, routes, gate_q, up_weight, down_weight, out_weight, cotangent):
    groups = lax.axis_size("expert")
    tokens, width = latent.shape
    unit = up_weight.shape[2]
    count = groups * ROWS
    half = shape(tokens, width // 2)
    half_wide = shape(tokens, width // 2, dtype=F32)
    me = (2 * (lax.axis_index("z") & 1) + lax.axis_index("core")).astype(jnp.int32).reshape(1)
    table = jnp.concatenate([routes, gate_q], axis=1).T

    coef = call(pick_kernel, shape(count, tokens), me, table, scalars=1)
    packs = call(
        pack_kernel,
        [shape(2 * width, unit)] * (QUAD - 1),
        me, up_weight, down_weight, scalars=1,
    )
    packs = [swap(p, d) for d, p in enumerate(packs, 1)]

    back = call(
        back_kernel, [half_wide, half], me, cotangent, out_weight,
        scalars=1, flops=2 * tokens * width * cotangent.shape[1], in_hbm=(1, 2), vmem=BACK_VMEM,
        scratch=[
            pltpu.VMEM(cotangent.shape, BF16),
            pltpu.VMEM(out_weight.shape, BF16),
            pltpu.SemaphoreType.DMA((2,)),
        ],
    )
    *back, table, coef = sum_over_head(*back, beside=(table, coef))
    send = call(
        send_kernel,
        shape(count, width),
        me, table, coef, latent, *back,
        scalars=1, out_hbm=(0,), vmem=SEND_VMEM,
        scratch=[pltpu.VMEM((count, width), BF16), pltpu.SemaphoreType.DMA((CHUNKS,))],
    )
    rows = exchange(send, "expert")
    hidden = unit * QUAD
    copies = 2 * QUAD + 1 + (QUAD - 1) * (width // unit)
    up_space, down_space = pltpu.VMEM((width, hidden), BF16), pltpu.VMEM((hidden, width), BF16)
    out = call(
        forward_kernel,
        shape(count, width // 2),
        me, rows, up_weight, down_weight, *packs,
        scalars=1, flops=4 * count * width * hidden,
        in_hbm=range(2, 4 + QUAD), out_hbm=(0,), vmem=FORWARD_VMEM,
        scratch=[
            up_space, down_space,
            pltpu.VMEM((count, width // 2), BF16), pltpu.SemaphoreType.DMA((copies,)),
        ],
    )
    grads = call(
        weight_kernel,
        [shape(width, unit)] * QUAD,
        me, rows, up_weight, down_weight, *packs,
        scalars=1, flops=6 * count * width * hidden,
        in_hbm=range(2, 4 + QUAD), out_hbm=range(QUAD), vmem=WEIGHT_VMEM,
        scratch=[up_space, down_space, up_space, pltpu.SemaphoreType.DMA((copies + QUAD,))],
    )
    grads = [grads[0]] + [swap(g, d, back=True) for d, g in enumerate(grads[1:], 1)]
    returned, *grads[1:3] = lax.optimization_barrier((exchange(out, "expert"), *grads[1:3]))
    grad_up = call(grad_kernel, shape(*up_weight.shape), me, *grads, scalars=1)
    comb = call(combine_kernel, [half_wide, half], me, returned, coef, gate_q, scalars=1)
    comb = sum_over_head(*comb)
    mixed = call(
        mixed_kernel, shape(tokens, out_weight.shape[1]), me, *comb, out_weight,
        scalars=1, flops=2 * tokens * width * out_weight.shape[1],
    )
    return (mixed, grad_up)


def solution(mesh):
    groups, members = mesh.devices.shape
    fine = Mesh(mesh.devices.reshape(groups, members // 2, 2), ("expert", *HEAD))
    placed = (
        P("expert", None),
        P("expert", None),
        P("expert", None),
        P("expert", None, HEAD),
        P("expert", HEAD, None),
        P(None, HEAD),
        P("expert", HEAD),
    )
    return jax.shard_map(
        per_device,
        mesh=fine,
        in_specs=placed,
        out_specs=(P("expert", HEAD), P("expert", None, HEAD)),
        check_vma=False,
    )
```

profile of v0, /device:TPU:1, one launch (start us, length us, event | category | flops | bytes accessed | tf_op | source)
XLA Modules:
  0.0 138.5 jit_solution(2745056877545487509)
XLA Ops:
  0.6 0.7 copy-done.5
  1.4 1.0 copy-done.2
  2.4 0.3 shard_map.86
  2.7 16.1 %collective-permute-start = (bf16[32,512]{1,0:T(8,128)(2,1)S(1)}, bf16[32,512]{1,0:T(8,128)(2,1)S(1)}, u32[]{:S(2)}, u32[]{:S(2)}) collective-permute-start(bf16[32,512]{1,0:T(8,128)(2,1)S(1)} %get-tuple-element.20), channel_id=1, source_target_pairs={{0,1},{1,0},{2,3},{3,2},{4,5},{5,4},{6,7},{7,6},{8,9},{9,8},{10,11... | collective-permute-start | bytes 98312 | tf_op jit(solution)/shard_map/ppermute | solution.py:251
  18.8 0.8 collective-permute-done.got_ref
  19.6 0.7 shard_map.87
  20.4 3.9 %all-to-all-start = ((bf16[8,32,512]{2,1,0:T(8,128)(2,1)}), bf16[8,32,512]{2,1,0:T(8,128)(2,1)S(1)}, u32[]{:S(2)}, u32[]{:S(2)}) async-start(bf16[8,32,512]{2,1,0:T(8,128)(2,1)} %shard_map.87), calls=%async_computation | async-start | bytes 524288 | tf_op jit(solution)/shard_map/all_to_all | solution.py:257
  24.3 0.8 shard_map.88.coef_ref
  25.1 10.4 %all-to-all-done.i_ref = bf16[8,32,512]{2,1,0:T(8,128)(2,1)S(1)} async-done(((bf16[8,32,512]{2,1,0:T(8,128)(2,1)}), bf16[8,32,512]{2,1,0:T(8,128)(2,1)S(1)}, u32[]{:S(2)}, u32[]{:S(2)}) %all-to-all-start) | async-done | bytes 262176 | tf_op jit(solution)/shard_map/all_to_all | solution.py:257
  35.5 3.6 %collective-permute-start.1 = (bf16[32,512]{1,0:T(8,128)(2,1)S(1)}, bf16[32,512]{1,0:T(8,128)(2,1)S(1)}, u32[]{:S(2)}, u32[]{:S(2)}) collective-permute-start(bf16[32,512]{1,0:T(8,128)(2,1)S(1)} %shard_map.89.own_ref), channel_id=1, source_target_pairs={{0,1},{1,0},{2,3},{3,2},{4,5},{5,4},{6,7},{7,6},{8,9},{9,8},{10,11... | collective-permute-start | bytes 98312 | tf_op jit(solution)/shard_map/ppermute | solution.py:251
  39.1 0.8 collective-permute-done.1.other_ref
  39.9 0.0 copy-done.4
  39.9 1.4 %shard_map.90 = bf16[512,1024]{1,0:T(8,128)(2,1)} custom-call(s32[1]{0:T(128)} %bitcast.me_ref, s32[44,32]{1,0:T(8,128)S(1)} %add_bitcast_fusion.table_ref, bf16[512,32]{1,0:T(8,128)(2,1)S(1)} %shard_map.88.coef_ref, bf16[32,1024]{1,0:T(8,128)(2,1)S(1)} %copy-done.4, bf16[32,512]{1,0:T(8,128)(2,1)S(1)} %shard_map.89.own_ref, ...), custom_call_target="tpu_custom_call" | custom-call | bytes 338952 | tf_op jit(solution)/shard_map/pallas_call | solution.py:27
  41.3 0.0 copy-start
  41.3 0.0 copy-start.1
  41.4 13.3 %all-to-all-start.1 = ((bf16[64,8,1024]{2,1,0:T(8,128)(2,1)}), bf16[64,8,1024]{2,1,0:T(8,128)(2,1)S(1)}, u32[]{:S(2)}, u32[]{:S(2)}) async-start(bf16[64,8,1024]{2,1,0:T(8,128)(2,1)} %bitcast.10), calls=%async_computation.1 | async-start | bytes 2097152 | tf_op jit(solution)/shard_map/all_to_all | solution.py:240
  54.7 0.2 shard_map.91
  54.9 2.5 %collective-permute-start.2 = (bf16[2048,128]{1,0:T(8,128)(2,1)S(1)}, bf16[2048,128]{1,0:T(8,128)(2,1)S(1)}, u32[]{:S(2)}, u32[]{:S(2)}) collective-permute-start(bf16[2048,128]{1,0:T(8,128)(2,1)S(1)} %get-tuple-element.24), channel_id=1, source_target_pairs={{0,1},{1,0},{2,3},{3,2},{4,5},{5,4},{6,7},{7,6},{8,9},{9,8},{10,11... | collective-permute-start | bytes 1572872 | tf_op jit(solution)/shard_map/ppermute | solution.py:251
  57.5 2.2 %collective-permute-start.3 = (bf16[2048,128]{1,0:T(8,128)(2,1)S(1)}, bf16[2048,128]{1,0:T(8,128)(2,1)S(1)}, u32[]{:S(2)}, u32[]{:S(2)}) collective-permute-start(bf16[2048,128]{1,0:T(8,128)(2,1)S(1)} %get-tuple-element.25), channel_id=1, source_target_pairs={{0,14},{1,3},{2,0},{3,5},{4,2},{5,7},{6,4},{7,9},{8,6},{9,11},{10,... | collective-permute-start | bytes 1572872 | tf_op jit(solution)/shard_map/ppermute | solution.py:251
  59.7 3.3 %collective-permute-start.4 = (bf16[2048,128]{1,0:T(8,128)(2,1)S(1)}, bf16[2048,128]{1,0:T(8,128)(2,1)S(1)}, u32[]{:S(2)}, u32[]{:S(2)}) collective-permute-start(bf16[2048,128]{1,0:T(8,128)(2,1)S(1)} %get-tuple-element.26), channel_id=1, source_target_pairs={{0,15},{1,2},{2,1},{3,4},{4,3},{5,6},{6,5},{7,8},{8,7},{9,10},{10,... | collective-permute-start | bytes 1572872 | tf_op jit(solution)/shard_map/ppermute | solution.py:251
  62.9 0.0 collective-permute-done.2.refs_0_
  63.0 5.9 %collective-permute-done.3.refs_1_ = bf16[2048,128]{1,0:T(8,128)(2,1)S(1)} collective-permute-done((bf16[2048,128]{1,0:T(8,128)(2,1)S(1)}, bf16[2048,128]{1,0:T(8,128)(2,1)S(1)}, u32[]{:S(2)}, u32[]{:S(2)}) %collective-permute-start.3) | collective-permute-done | bytes 524320 | tf_op jit(solution)/shard_map/ppermute | solution.py:251
  68.9 4.9 %collective-permute-done.4.refs_2_ = bf16[2048,128]{1,0:T(8,128)(2,1)S(1)} collective-permute-done((bf16[2048,128]{1,0:T(8,128)(2,1)S(1)}, bf16[2048,128]{1,0:T(8,128)(2,1)S(1)}, u32[]{:S(2)}, u32[]{:S(2)}) %collective-permute-start.4) | collective-permute-done | bytes 524320 | tf_op jit(solution)/shard_map/ppermute | solution.py:251
  73.8 8.0 %all-to-all-done.1 = bf16[64,8,1024]{2,1,0:T(8,128)(2,1)S(1)} async-done(((bf16[64,8,1024]{2,1,0:T(8,128)(2,1)}), bf16[64,8,1024]{2,1,0:T(8,128)(2,1)S(1)}, u32[]{:S(2)}, u32[]{:S(2)}) %all-to-all-start.1) | async-done | bytes 1048608 | tf_op jit(solution)/shard_map/all_to_all | solution.py:240
  81.7 3.6 %shard_map.92 = bf16[512,512]{1,0:T(8,128)(2,1)} custom-call(s32[1]{0:T(128)} %bitcast.me_ref, bf16[512,1024]{1,0:T(8,128)(2,1)S(1)} %bitcast.7, bf16[4,1024,128]{2,1,0:T(8,128)(2,1)} %up_hbm.3, bf16[4,128,1024]{2,1,0:T(8,128)(2,1)} %down_hbm.3, bf16[2048,128]{1,0:T(8,128)(2,1)S(1)} %collective-permute-done.2.refs_0_, ...), custom_call_target="tpu_custom_call" | custom-call | flops 1073741824 | bytes 9437192 | tf_op jit(solution)/shard_map/pallas_call | solution.py:27
  85.3 8.8 %all-to-all-start.2 = ((bf16[64,8,512]{2,1,0:T(8,128)(2,1)}), bf16[64,8,512]{2,1,0:T(8,128)(2,1)S(1)}, u32[]{:S(2)}, u32[]{:S(2)}) async-start(bf16[64,8,512]{2,1,0:T(8,128)(2,1)} %bitcast.4), calls=%async_computation.2 | async-start | bytes 1048576 | tf_op jit(solution)/shard_map/all_to_all | solution.py:240
  94.1 4.4 %shard_map.93 = (bf16[1024,128]{1,0:T(8,128)(2,1)S(1)}, bf16[1024,128]{1,0:T(8,128)(2,1)}, bf16[1024,128]{1,0:T(8,128)(2,1)}, bf16[1024,128]{1,0:T(8,128)(2,1)S(1)}) custom-call(s32[1]{0:T(128)} %bitcast.me_ref, bf16[512,1024]{1,0:T(8,128)(2,1)S(1)} %bitcast.8, bf16[4,1024,128]{2,1,0:T(8,128)(2,1)} %up_hbm.3, bf16[4,128,1024]{2,1,0:T(8,128)(2,1)} %down_hbm.3, ...), custom_call_target="tpu_custom_call" | custom-call | flops 1610612736 | bytes 9437192 | tf_op jit(solution)/shard_map/pallas_call | solution.py:27
  98.6 0.7 copy-done.6
  99.3 3.4 %collective-permute-start.5 = (bf16[1024,128]{1,0:T(8,128)(2,1)}, bf16[1024,128]{1,0:T(8,128)(2,1)S(1)}, u32[]{:S(2)}, u32[]{:S(2)}) collective-permute-start(bf16[1024,128]{1,0:T(8,128)(2,1)} %get-tuple-element.27), channel_id=1, source_target_pairs={{1,0},{0,1},{3,2},{2,3},{5,4},{4,5},{7,6},{6,7},{9,8},{8,9},{11,10... | collective-permute-start | bytes 786440 | tf_op jit(solution)/shard_map/ppermute | solution.py:251
  102.7 1.9 %collective-permute-start.6 = (bf16[1024,128]{1,0:T(8,128)(2,1)}, bf16[1024,128]{1,0:T(8,128)(2,1)S(1)}, u32[]{:S(2)}, u32[]{:S(2)}) collective-permute-start(bf16[1024,128]{1,0:T(8,128)(2,1)} %get-tuple-element.28), channel_id=1, source_target_pairs={{14,0},{3,1},{0,2},{5,3},{2,4},{7,5},{4,6},{9,7},{6,8},{11,9},{8,1... | collective-permute-start | bytes 786440 | tf_op jit(solution)/shard_map/ppermute | solution.py:251
  104.6 0.1 copy.9.gate_ref
  104.7 0.0 collective-permute-done.5.refs_1_
  104.7 5.6 %collective-permute-done.6.refs_2_ = bf16[1024,128]{1,0:T(8,128)(2,1)S(1)} collective-permute-done((bf16[1024,128]{1,0:T(8,128)(2,1)}, bf16[1024,128]{1,0:T(8,128)(2,1)S(1)}, u32[]{:S(2)}, u32[]{:S(2)}) %collective-permute-start.6) | collective-permute-done | bytes 262176 | tf_op jit(solution)/shard_map/ppermute | solution.py:251
  110.3 0.0 all-to-all-done.2
  110.3 0.3 shard_map.94
  110.6 5.9 %collective-permute-start.7 = (bf16[32,512]{1,0:T(8,128)(2,1)S(1)}, bf16[32,512]{1,0:T(8,128)(2,1)S(1)}, u32[]{:S(2)}, u32[]{:S(2)}) collective-permute-start(bf16[32,512]{1,0:T(8,128)(2,1)S(1)} %get-tuple-element.31), channel_id=1, source_target_pairs={{0,1},{1,0},{2,3},{3,2},{4,5},{5,4},{6,7},{7,6},{8,9},{9,8},{10,11... | collective-permute-start | bytes 98312 | tf_op jit(solution)/shard_map/ppermute | solution.py:251
  116.6 0.8 collective-permute-done.7.got_ref
  117.4 0.7 shard_map.95
  118.1 3.5 %all-to-all-start.3 = ((bf16[8,32,512]{2,1,0:T(8,128)(2,1)}), bf16[8,32,512]{2,1,0:T(8,128)(2,1)S(1)}, u32[]{:S(2)}, u32[]{:S(2)}) async-start(bf16[8,32,512]{2,1,0:T(8,128)(2,1)} %shard_map.95), calls=%async_computation.3 | async-start | bytes 524288 | tf_op jit(solution)/shard_map/all_to_all | solution.py:257
  121.7 3.8 %collective-permute-start.9 = (bf16[1024,128]{1,0:T(8,128)(2,1)S(1)}, bf16[1024,128]{1,0:T(8,128)(2,1)S(1)}, u32[]{:S(2)}, u32[]{:S(2)}) collective-permute-start(bf16[1024,128]{1,0:T(8,128)(2,1)S(1)} %copy-done.7), channel_id=1, source_target_pairs={{15,0},{2,1},{1,2},{4,3},{3,4},{6,5},{5,6},{8,7},{7,8},{10,9},{9,1... | collective-permute-start | bytes 786440 | tf_op jit(solution)/shard_map/ppermute | solution.py:251
  125.5 8.3 %all-to-all-done.3.i_ref = bf16[8,32,512]{2,1,0:T(8,128)(2,1)S(1)} async-done(((bf16[8,32,512]{2,1,0:T(8,128)(2,1)}), bf16[8,32,512]{2,1,0:T(8,128)(2,1)S(1)}, u32[]{:S(2)}, u32[]{:S(2)}) %all-to-all-start.3) | async-done | bytes 262176 | tf_op jit(solution)/shard_map/all_to_all | solution.py:257
  133.8 2.6 %collective-permute-start.8 = (bf16[32,512]{1,0:T(8,128)(2,1)S(1)}, bf16[32,512]{1,0:T(8,128)(2,1)S(1)}, u32[]{:S(2)}, u32[]{:S(2)}) collective-permute-start(bf16[32,512]{1,0:T(8,128)(2,1)S(1)} %shard_map.96.own_ref), channel_id=1, source_target_pairs={{0,1},{1,0},{2,3},{3,2},{4,5},{5,4},{6,7},{7,6},{8,9},{9,8},{10,11... | collective-permute-start | bytes 98312 | tf_op jit(solution)/shard_map/ppermute | solution.py:251
  136.5 0.0 collective-permute-done.9.refs_3_
  136.5 0.0 copy-start.3
  136.5 1.0 shard_map.98
  137.5 0.0 collective-permute-done.8.other_ref
  137.5 0.1 copy-done.3
  137.6 0.8 shard_map.97
  (15 shorter events, 0.1 us)
Async XLA Ops:
  0.6 0.7 copy-start.5
  1.3 1.0 copy-start.2
  2.7 16.9 %collective-permute-start = (bf16[32,512]{1,0:T(8,128)(2,1)S(1)}, bf16[32,512]{1,0:T(8,128)(2,1)S(1)}, u32[]{:S(2)}, u32[]{:S(2)}) collective-permute-start(bf16[32,512]{1,0:T(8,128)(2,1)S(1)} %get-tuple-element.20), channel_id=1, source_target_pairs={{0,1},{1,0},{2,3},{3,2},{4,5},{5,4},{6,7},{7,6},{8,9},{9,8},{10,11... | collective-permute-start | bytes 98312 | tf_op jit(solution)/shard_map/ppermute | solution.py:251
  20.4 3.9 %copy-start.8 = (s32[32,22]{0,1:T(8,128)S(1)}, s32[32,22]{0,1:T(8,128)}, u32[]{:S(2)}) copy-start(s32[32,22]{0,1:T(8,128)} %param.9) | copy-start | bytes 8452
  20.4 3.9 %copy-start.9 = (s32[32,22]{0,1:T(8,128)S(1)}, s32[32,22]{0,1:T(8,128)}, u32[]{:S(2)}) copy-start(s32[32,22]{0,1:T(8,128)} %param.8) | copy-start | bytes 8452
  20.4 15.1 %all-to-all-start = ((bf16[8,32,512]{2,1,0:T(8,128)(2,1)}), bf16[8,32,512]{2,1,0:T(8,128)(2,1)S(1)}, u32[]{:S(2)}, u32[]{:S(2)}) async-start(bf16[8,32,512]{2,1,0:T(8,128)(2,1)} %shard_map.87), calls=%async_computation | async-start | bytes 524288 | tf_op jit(solution)/shard_map/all_to_all | solution.py:257
  25.1 14.8 %copy-start.4 = (bf16[32,1024]{1,0:T(8,128)(2,1)S(1)}, bf16[32,1024]{1,0:T(8,128)(2,1)}, u32[]{:S(2)}) copy-start(bf16[32,1024]{1,0:T(8,128)(2,1)} %latent_ref.1) | copy-start | bytes 196612
  35.5 4.4 %collective-permute-start.1 = (bf16[32,512]{1,0:T(8,128)(2,1)S(1)}, bf16[32,512]{1,0:T(8,128)(2,1)S(1)}, u32[]{:S(2)}, u32[]{:S(2)}) collective-permute-start(bf16[32,512]{1,0:T(8,128)(2,1)S(1)} %shard_map.89.own_ref), channel_id=1, source_target_pairs={{0,1},{1,0},{2,3},{3,2},{4,5},{5,4},{6,7},{7,6},{8,9},{9,8},{10,11... | collective-permute-start | bytes 98312 | tf_op jit(solution)/shard_map/ppermute | solution.py:251
  41.3 13.4 %copy-start = (bf16[4,1024,128]{2,1,0:T(8,128)(2,1)S(1)}, bf16[4,1024,128]{2,1,0:T(8,128)(2,1)}, u32[]{:S(2)}) copy-start(bf16[4,1024,128]{2,1,0:T(8,128)(2,1)} %up_hbm.3) | copy-start | bytes 3145732
  41.3 13.4 %copy-start.1 = (bf16[4,128,1024]{2,1,0:T(8,128)(2,1)S(1)}, bf16[4,128,1024]{2,1,0:T(8,128)(2,1)}, u32[]{:S(2)}) copy-start(bf16[4,128,1024]{2,1,0:T(8,128)(2,1)} %down_hbm.3) | copy-start | bytes 3145732
  41.4 40.4 %all-to-all-start.1 = ((bf16[64,8,1024]{2,1,0:T(8,128)(2,1)}), bf16[64,8,1024]{2,1,0:T(8,128)(2,1)S(1)}, u32[]{:S(2)}, u32[]{:S(2)}) async-start(bf16[64,8,1024]{2,1,0:T(8,128)(2,1)} %bitcast.10), calls=%async_computation.1 | async-start | bytes 2097152 | tf_op jit(solution)/shard_map/all_to_all | solution.py:240
  54.9 8.0 %collective-permute-start.2 = (bf16[2048,128]{1,0:T(8,128)(2,1)S(1)}, bf16[2048,128]{1,0:T(8,128)(2,1)S(1)}, u32[]{:S(2)}, u32[]{:S(2)}) collective-permute-start(bf16[2048,128]{1,0:T(8,128)(2,1)S(1)} %get-tuple-element.24), channel_id=1, source_target_pairs={{0,1},{1,0},{2,3},{3,2},{4,5},{5,4},{6,7},{7,6},{8,9},{9,8},{10,11... | collective-permute-start | bytes 1572872 | tf_op jit(solution)/shard_map/ppermute | solution.py:251
  57.5 11.4 %collective-permute-start.3 = (bf16[2048,128]{1,0:T(8,128)(2,1)S(1)}, bf16[2048,128]{1,0:T(8,128)(2,1)S(1)}, u32[]{:S(2)}, u32[]{:S(2)}) collective-permute-start(bf16[2048,128]{1,0:T(8,128)(2,1)S(1)} %get-tuple-element.25), channel_id=1, source_target_pairs={{0,14},{1,3},{2,0},{3,5},{4,2},{5,7},{6,4},{7,9},{8,6},{9,11},{10,... | collective-permute-start | bytes 1572872 | tf_op jit(solution)/shard_map/ppermute | solution.py:251
  59.7 14.1 %collective-permute-start.4 = (bf16[2048,128]{1,0:T(8,128)(2,1)S(1)}, bf16[2048,128]{1,0:T(8,128)(2,1)S(1)}, u32[]{:S(2)}, u32[]{:S(2)}) collective-permute-start(bf16[2048,128]{1,0:T(8,128)(2,1)S(1)} %get-tuple-element.26), channel_id=1, source_target_pairs={{0,15},{1,2},{2,1},{3,4},{4,3},{5,6},{6,5},{7,8},{8,7},{9,10},{10,... | collective-permute-start | bytes 1572872 | tf_op jit(solution)/shard_map/ppermute | solution.py:251
  85.3 25.0 %all-to-all-start.2 = ((bf16[64,8,512]{2,1,0:T(8,128)(2,1)}), bf16[64,8,512]{2,1,0:T(8,128)(2,1)S(1)}, u32[]{:S(2)}, u32[]{:S(2)}) async-start(bf16[64,8,512]{2,1,0:T(8,128)(2,1)} %bitcast.4), calls=%async_computation.2 | async-start | bytes 1048576 | tf_op jit(solution)/shard_map/all_to_all | solution.py:240
  98.5 0.7 copy-start.6
  99.3 5.4 %collective-permute-start.5 = (bf16[1024,128]{1,0:T(8,128)(2,1)}, bf16[1024,128]{1,0:T(8,128)(2,1)S(1)}, u32[]{:S(2)}, u32[]{:S(2)}) collective-permute-start(bf16[1024,128]{1,0:T(8,128)(2,1)} %get-tuple-element.27), channel_id=1, source_target_pairs={{1,0},{0,1},{3,2},{2,3},{5,4},{4,5},{7,6},{6,7},{9,8},{8,9},{11,10... | collective-permute-start | bytes 786440 | tf_op jit(solution)/shard_map/ppermute | solution.py:251
  102.7 7.6 %collective-permute-start.6 = (bf16[1024,128]{1,0:T(8,128)(2,1)}, bf16[1024,128]{1,0:T(8,128)(2,1)S(1)}, u32[]{:S(2)}, u32[]{:S(2)}) collective-permute-start(bf16[1024,128]{1,0:T(8,128)(2,1)} %get-tuple-element.28), channel_id=1, source_target_pairs={{14,0},{3,1},{0,2},{5,3},{2,4},{7,5},{4,6},{9,7},{6,8},{11,9},{8,1... | collective-permute-start | bytes 786440 | tf_op jit(solution)/shard_map/ppermute | solution.py:251
  110.6 6.8 %collective-permute-start.7 = (bf16[32,512]{1,0:T(8,128)(2,1)S(1)}, bf16[32,512]{1,0:T(8,128)(2,1)S(1)}, u32[]{:S(2)}, u32[]{:S(2)}) collective-permute-start(bf16[32,512]{1,0:T(8,128)(2,1)S(1)} %get-tuple-element.31), channel_id=1, source_target_pairs={{0,1},{1,0},{2,3},{3,2},{4,5},{5,4},{6,7},{7,6},{8,9},{9,8},{10,11... | collective-permute-start | bytes 98312 | tf_op jit(solution)/shard_map/ppermute | solution.py:251
  118.1 3.6 %copy-start.7 = (bf16[1024,128]{1,0:T(8,128)(2,1)S(1)}, bf16[1024,128]{1,0:T(8,128)(2,1)}, u32[]{:S(2)}) copy-start(bf16[1024,128]{1,0:T(8,128)(2,1)} %copy-done.6) | copy-start | bytes 786436
  118.1 15.7 %all-to-all-start.3 = ((bf16[8,32,512]{2,1,0:T(8,128)(2,1)}), bf16[8,32,512]{2,1,0:T(8,128)(2,1)S(1)}, u32[]{:S(2)}, u32[]{:S(2)}) async-start(bf16[8,32,512]{2,1,0:T(8,128)(2,1)} %shard_map.95), calls=%async_computation.3 | async-start | bytes 524288 | tf_op jit(solution)/shard_map/all_to_all | solution.py:257
  121.7 14.8 %collective-permute-start.9 = (bf16[1024,128]{1,0:T(8,128)(2,1)S(1)}, bf16[1024,128]{1,0:T(8,128)(2,1)S(1)}, u32[]{:S(2)}, u32[]{:S(2)}) collective-permute-start(bf16[1024,128]{1,0:T(8,128)(2,1)S(1)} %copy-done.7), channel_id=1, source_target_pairs={{15,0},{2,1},{1,2},{4,3},{3,4},{6,5},{5,6},{8,7},{7,8},{10,9},{9,1... | collective-permute-start | bytes 786440 | tf_op jit(solution)/shard_map/ppermute | solution.py:251
  133.8 3.7 %collective-permute-start.8 = (bf16[32,512]{1,0:T(8,128)(2,1)S(1)}, bf16[32,512]{1,0:T(8,128)(2,1)S(1)}, u32[]{:S(2)}, u32[]{:S(2)}) collective-permute-start(bf16[32,512]{1,0:T(8,128)(2,1)S(1)} %shard_map.96.own_ref), channel_id=1, source_target_pairs={{0,1},{1,0},{2,3},{3,2},{4,5},{5,4},{6,7},{7,6},{8,9},{9,8},{10,11... | collective-permute-start | bytes 98312 | tf_op jit(solution)/shard_map/ppermute | solution.py:251
  136.5 1.2 copy-start.3
where the time goes:
time: 139 us; the launch traced here: 138 us
  starting transfers between devices  74.8 us (54%)
  waiting for transfers between devices  45.6 us (33%)
  Pallas kernels  14.4 us (10%)
  local copies, waits for them, and re-layouts  2.7 us (2%)
    ppermute x10, starting transfers between devices, swap(): lax.ppermute(array, HEAD, [(b, a) for a, b in pairs] if back else pairs)  45.2 us
    all_to_all x2, starting transfers between devices, exchange(): moved = lax.all_to_all(split, axis, split_axis=0, concat_axis=0, tiled=True)  22.2 us
    ppermute x10, waiting for transfers between devices, swap(): lax.ppermute(array, HEAD, [(b, a) for a, b in pairs] if back else pairs)  19 us
    all_to_all x2, waiting for transfers between devices, sum_over_head(): moved = lax.all_to_all(spread, 'z', split_axis=0, concat_axis=0, tiled=True)  18.7 us
    pallas_call x13, Pallas kernels, call(): pl.pallas_call(kernel, out_shape=outs, in_specs=ins, out_specs=places[0]...  14.4 us
    all_to_all x2, waiting for transfers between devices, exchange(): moved = lax.all_to_all(split, axis, split_axis=0, concat_axis=0, tiled=True)  7.96 us
    all_to_all x2, starting transfers between devices, sum_over_head(): moved = lax.all_to_all(spread, 'z', split_axis=0, concat_axis=0, tiled=True)  7.43 us
  transfers between devices with their start and end apart: 14, of which 9 were waited for; matrix products, arithmetic and copies ran while one was open for 0% of the time, Pallas kernels for 5%

commit v1 on v0

--- a/solution.py
+++ b/solution.py
@@ -81,46 +81,61 @@
     o_ref[...] = jnp.sum(i_ref[...].astype(F32), axis=0).astype(BF16)
 
 
-def pick_kernel(me_ref, table_ref, coef_ref):
-    count, tokens = coef_ref.shape
+def pick_kernel(me_ref, table_ref, *coef_refs):
+    count, tokens = coef_refs[0].shape
     top = table_ref.shape[0] // 2
     row = lax.broadcasted_iota(jnp.int32, (count, tokens), 0)
-    expert = QUAD * (row // ROWS) + me_ref[0]
-    score = jnp.zeros((count, tokens), jnp.int32)
-    for k in range(top):
-        q = table_ref[top + k : top + k + 1, :]
-        score = score + jnp.where(table_ref[k : k + 1, :] == expert, q, 0)
-    score = score.astype(F32)
-    named = score > 0.0
     earlier = lax.broadcasted_iota(jnp.int32, (tokens, tokens), 0)
     later = lax.broadcasted_iota(jnp.int32, (tokens, tokens), 1)
     before = jnp.where(earlier < later, 1.0, 0.0).astype(BF16)
-    rank = dot(jnp.where(named, 1.0, 0.0).astype(BF16), before, ((1,), (0,)))
-    here = named & (rank == (row % MOST).astype(F32))
-    coef_ref[...] = jnp.where(here, score, 0.0).astype(BF16)
-
-
-def send_kernel(me_ref, table_ref, coef_ref, latent_ref, own_ref, other_ref, send_ref, buf, sems):
-    count = send_ref.shape[0]
+    coefs = []
+    for core in range(2):
+        expert = QUAD * (row // ROWS) + (me_ref[0] - me_ref[0] % 2 + core)
+        score = jnp.zeros((count, tokens), jnp.int32)
+        for k in range(top):
+            q = table_ref[top + k : top + k + 1, :]
+            score = score + jnp.where(table_ref[k : k + 1, :] == expert, q, 0)
+        score = score.astype(F32)
+        named = score > 0.0
+        rank = dot(jnp.where(named, 1.0, 0.0).astype(BF16), before, ((1,), (0,)))
+        here = named & (rank == (row % MOST).astype(F32))
+        coefs.append(jnp.where(here, score, 0.0))
+    first = me_ref[0] % 2 == 0
+    for ref, coef in zip(coef_refs, [jnp.where(first, *coefs), *coefs]):
+        ref[...] = coef.astype(BF16)
+
+
+def send_kernel(table_ref, coef_ref, coef0_ref, coef1_ref, latent_ref, half_ref, send_ref, buf, sems):
+    count, width = send_ref.shape
+    half = width // 2
     top = table_ref.shape[0] // 2
     step = count // CHUNKS
-    back = joined(me_ref, own_ref[...], other_ref[...]).astype(BF16)
+    back = half_ref[...]
     latent = latent_ref[...]
     total = jnp.sum(table_ref[top:, :].astype(F32), axis=0, keepdims=True)
     is_latent = lax.broadcasted_iota(jnp.int32, (step, 1), 0) % ROWS < MOST
     copies = []
     for i in range(CHUNKS):
         at = pl.ds(step * i, step)
-        coef = coef_ref[at, :].astype(F32)
-        gate = jnp.sum(coef / total, axis=1, keepdims=True)
-        pick = jnp.where(coef > 0.0, 1.0, 0.0).astype(BF16)
+        pick = jnp.where(coef_ref[at, :].astype(F32) > 0.0, 1.0, 0.0).astype(BF16)
         latent_rows = dot(pick, latent, ((1,), (0,)))
-        back_rows = dot(pick, back, ((1,), (0,)))
-        buf[at, :] = jnp.where(is_latent, latent_rows, gate * back_rows).astype(BF16)
+        for core, ref in enumerate((coef0_ref, coef1_ref)):
+            coef = ref[at, :].astype(F32)
+            gate = jnp.sum(coef / total, axis=1, keepdims=True)
+            pick = jnp.where(coef > 0.0, 1.0, 0.0).astype(BF16)
+            rows = gate * dot(pick, back, ((1,), (0,)))
+            columns = slice(half * core, half * core + half)
+            buf[at, columns] = jnp.where(is_latent, latent_rows[:, columns], rows).astype(BF16)
         copies.append(pltpu.make_async_copy(buf.at[at, :], send_ref.at[at, :], sems.at[i]))
         copies[-1].start()
     for copy in copies:
         copy.wait()
+
+
+def other_kernel(me_ref, rows_ref, o_ref):
+    half = o_ref.shape[1]
+    first = me_ref[0] % 2 == 0
+    o_ref[...] = jnp.where(first, rows_ref[:, half:], rows_ref[:, :half])
 
 
 def pack_kernel(me_ref, up_ref, down_ref, *outs):
@@ -190,7 +205,7 @@
     wait([copies.start(out_ref, out_hbm)])
 
 
-def weight_kernel(me_ref, rows_ref, up_hbm, down_hbm, *refs):
+def weight_kernel(me_ref, rows_ref, got_ref, up_hbm, down_hbm, *refs):
     packs, refs = refs[: QUAD - 1], refs[QUAD - 1 :]
     outs_hbm, refs = refs[:QUAD], refs[QUAD:]
     up_ref, down_ref, grad_ref, sems = refs
@@ -203,7 +218,13 @@
     rows = rows_ref[...]
     act = jnp.maximum(dot(rows, up_ref[...], ((1,), (0,))), 0.0)
     wait(downs)
-    hidden_grad = pltpu.roll(dot(rows, down_ref[...], ((1,), (1,))), count - MOST, 0)
+    half = got_ref.shape[1]
+    first = me_ref[0] % 2 == 0
+    own, got = jnp.where(first, rows[:, :half], rows[:, half:]), got_ref[...]
+    grads = (jnp.where(first, own, got), jnp.where(first, got, own))
+    hidden_grad = dot(grads[0], down_ref[:, :half], ((1,), (1,)))
+    hidden_grad = hidden_grad + dot(grads[1], down_ref[:, half:], ((1,), (1,)))
+    hidden_grad = pltpu.roll(hidden_grad, count - MOST, 0)
     pre_grad = jnp.where(latent_rows_of(count), hidden_grad * 2.0 * act, 0.0).astype(BF16)
     grad_ref[...] = dot(rows, pre_grad, ((0,), (0,))).astype(BF16)
     wait([copies.start(grad_ref.at[:, pl.ds(unit * d, unit)], o) for d, o in enumerate(outs_hbm)])
@@ -256,8 +277,7 @@
     spread = call(spread_kernel, shape(chips, *keep.shape), keep, swap(give, 1))
     moved = lax.all_to_all(spread, "z", split_axis=0, concat_axis=0, tiled=True)
     moved, *beside = lax.optimization_barrier((moved, *beside))
-    own = call(sum_kernel, shape(*keep.shape), moved)
-    return own, swap(own, 1), *beside
+    return call(sum_kernel, shape(*keep.shape), moved), *beside
 
 
 def per_device(latent, routes, gate_q, up_weight, down_weight, out_weight, cotangent):
@@ -270,7 +290,7 @@
     me = (2 * (lax.axis_index("z") & 1) + lax.axis_index("core")).astype(jnp.int32).reshape(1)
     table = jnp.concatenate([routes, gate_q], axis=1).T
 
-    coef = call(pick_kernel, shape(count, tokens), me, table, scalars=1)
+    coefs = call(pick_kernel, [shape(count, tokens)] * 3, me, table, scalars=1)
     packs = call(
         pack_kernel,
         [shape(2 * width, unit)] * (QUAD - 1),
@@ -287,12 +307,12 @@
             pltpu.SemaphoreType.DMA((2,)),
         ],
     )
-    *back, table, coef = sum_over_head(*back, beside=(table, coef))
+    back, table, *coefs = sum_over_head(*back, beside=(table, *coefs))
     send = call(
         send_kernel,
         shape(count, width),
-        me, table, coef, latent, *back,
-        scalars=1, out_hbm=(0,), vmem=SEND_VMEM,
+        table, *coefs, latent, back,
+        out_hbm=(0,), vmem=SEND_VMEM,
         scratch=[pltpu.VMEM((count, width), BF16), pltpu.SemaphoreType.DMA((CHUNKS,))],
     )
     rows = exchange(send, "expert")
@@ -310,21 +330,23 @@
             pltpu.VMEM((count, width // 2), BF16), pltpu.SemaphoreType.DMA((copies,)),
         ],
     )
+    rows, out = lax.optimization_barrier((rows, out))
+    got = swap(call(other_kernel, shape(count, width // 2), me, rows, scalars=1), 1)
     grads = call(
         weight_kernel,
         [shape(width, unit)] * QUAD,
-        me, rows, up_weight, down_weight, *packs,
+        me, rows, got, up_weight, down_weight, *packs,
         scalars=1, flops=6 * count * width * hidden,
-        in_hbm=range(2, 4 + QUAD), out_hbm=range(QUAD), vmem=WEIGHT_VMEM,
+        in_hbm=range(3, 5 + QUAD), out_hbm=range(QUAD), vmem=WEIGHT_VMEM,
         scratch=[up_space, down_space, up_space, pltpu.SemaphoreType.DMA((copies + QUAD,))],
     )
     grads = [grads[0]] + [swap(g, d, back=True) for d, g in enumerate(grads[1:], 1)]
     returned, *grads[1:3] = lax.optimization_barrier((exchange(out, "expert"), *grads[1:3]))
     grad_up = call(grad_kernel, shape(*up_weight.shape), me, *grads, scalars=1)
-    comb = call(combine_kernel, [half_wide, half], me, returned, coef, gate_q, scalars=1)
-    comb = sum_over_head(*comb)
+    comb = call(combine_kernel, [half_wide, half], me, returned, coefs[0], gate_q, scalars=1)
+    (comb,) = sum_over_head(*comb)
     mixed = call(
-        mixed_kernel, shape(tokens, out_weight.shape[1]), me, *comb, out_weight,
+        mixed_kernel, shape(tokens, out_weight.shape[1]), me, comb, swap(comb, 1), out_weight,
         scalars=1, flops=2 * tokens * width * out_weight.shape[1],
     )
     return (mixed, grad_up)

time: 139 us -> 138 us (level)
  Pallas kernels: 14.4 us -> 16.5 us
  waiting for transfers between devices: 45.6 us -> 43.6 us
    pallas_call x13 -> x14, Pallas kernels: 14.4 us -> 16.5 us  [call(): pl.pallas_call(kernel, out_shape=outs, in_specs=ins, out_specs=places[0]...]
    all_to_all x2, waiting for transfers between devices: 7.96 us -> 5.91 us  [exchange(): moved = lax.all_to_all(split, axis, split_axis=0, concat_axis=0, tiled=True)]
    ppermute x10, starting transfers between devices: 45.2 us -> 43.5 us  [swap(): lax.ppermute(array, HEAD, [(b, a) for a, b in pairs] if back else pairs)]
    unnamed x21 -> x19, local copies, waits for them, and re-layouts: 2.7 us -> 2.78 us
  transfers between devices with their start and end apart: 14 -> 14, of which waited for: 9 -> 9; matrix products, arithmetic and copies ran while one was open for 0% -> 0% of each run, Pallas kernels for 5% -> 6%
where the time goes in v1:
time: 138 us; the launch traced here: 137 us
  starting transfers between devices  73.6 us (53%)
  waiting for transfers between devices  43.6 us (32%)
  Pallas kernels  16.5 us (12%)
  local copies, waits for them, and re-layouts  2.78 us (2%)
    ppermute x10, starting transfers between devices, swap(): lax.ppermute(array, HEAD, [(b, a) for a, b in pairs] if back else pairs)  43.5 us
    all_to_all x2, starting transfers between devices, exchange(): moved = lax.all_to_all(split, axis, split_axis=0, concat_axis=0, tiled=True)  22.8 us
    ppermute x10, waiting for transfers between devices, swap(): lax.ppermute(array, HEAD, [(b, a) for a, b in pairs] if back else pairs)  19.6 us
    all_to_all x2, waiting for transfers between devices, sum_over_head(): moved = lax.all_to_all(spread, 'z', split_axis=0, concat_axis=0, tiled=True)  18.1 us
    pallas_call x14, Pallas kernels, call(): pl.pallas_call(kernel, out_shape=outs, in_specs=ins, out_specs=places[0]...  16.5 us
    all_to_all x2, starting transfers between devices, sum_over_head(): moved = lax.all_to_all(spread, 'z', split_axis=0, concat_axis=0, tiled=True)  7.3 us
    all_to_all x2, waiting for transfers between devices, exchange(): moved = lax.all_to_all(split, axis, split_axis=0, concat_axis=0, tiled=True)  5.91 us
    unnamed x19, local copies, waits for them, and re-layouts  2.78 us
  transfers between devices with their start and end apart: 14, of which 9 were waited for; matrix products, arithmetic and copies ran while one was open for 0% of the time, Pallas kernels for 6%

profile of v1, /device:TPU:1, one launch (start us, length us, event | category | flops | bytes accessed | tf_op | source)
XLA Modules:
  0.0 137.3 jit_solution(12683378616515175777)
XLA Ops:
  0.6 0.7 copy-done.6
  1.4 1.0 copy-done.3
  2.4 0.3 shard_map.86
  2.7 16.1 %collective-permute-start = (bf16[32,512]{1,0:T(8,128)(2,1)S(1)}, bf16[32,512]{1,0:T(8,128)(2,1)S(1)}, u32[]{:S(2)}, u32[]{:S(2)}) collective-permute-start(bf16[32,512]{1,0:T(8,128)(2,1)S(1)} %get-tuple-element.27), channel_id=1, source_target_pairs={{0,1},{1,0},{2,3},{3,2},{4,5},{5,4},{6,7},{7,6},{8,9},{9,8},{10,11... | collective-permute-start | bytes 98312 | tf_op jit(solution)/shard_map/ppermute | solution.py:272
  18.8 0.8 collective-permute-done.got_ref
  19.6 0.7 shard_map.87
  20.4 3.9 %all-to-all-start = ((bf16[8,32,512]{2,1,0:T(8,128)(2,1)}), bf16[8,32,512]{2,1,0:T(8,128)(2,1)S(1)}, u32[]{:S(2)}, u32[]{:S(2)}) async-start(bf16[8,32,512]{2,1,0:T(8,128)(2,1)} %shard_map.87), calls=%async_computation | async-start | bytes 524288 | tf_op jit(solution)/shard_map/all_to_all | solution.py:278
  24.3 1.4 %shard_map.88 = (bf16[512,32]{1,0:T(8,128)(2,1)S(1)}, bf16[512,32]{1,0:T(8,128)(2,1)S(1)}, bf16[512,32]{1,0:T(8,128)(2,1)S(1)}) custom-call(s32[1]{0:T(128)} %bitcast.me_ref, s32[44,32]{1,0:T(8,128)S(1)} %add_bitcast_fusion.table_ref), custom_call_target="tpu_custom_call" | custom-call | bytes 11272 | tf_op jit(solution)/shard_map/pallas_call | solution.py:27
  25.7 9.7 %all-to-all-done.i_ref = bf16[8,32,512]{2,1,0:T(8,128)(2,1)S(1)} async-done(((bf16[8,32,512]{2,1,0:T(8,128)(2,1)}), bf16[8,32,512]{2,1,0:T(8,128)(2,1)S(1)}, u32[]{:S(2)}, u32[]{:S(2)}) %all-to-all-start) | async-done | bytes 262176 | tf_op jit(solution)/shard_map/all_to_all | solution.py:278
  35.5 0.8 copy-done.5
  36.3 1.4 %shard_map.90 = bf16[512,1024]{1,0:T(8,128)(2,1)} custom-call(s32[44,32]{1,0:T(8,128)S(1)} %add_bitcast_fusion.table_ref, bf16[512,32]{1,0:T(8,128)(2,1)S(1)} %get-tuple-element.32.coef_ref, bf16[512,32]{1,0:T(8,128)(2,1)S(1)} %get-tuple-element.33.coef0_ref, bf16[512,32]{1,0:T(8,128)(2,1)S(1)} %get-tuple-element.34.coef1_ref, ...), custom_call_target="tpu_custom_call" | custom-call | bytes 404480 | tf_op jit(solution)/shard_map/pallas_call | solution.py:27
  37.7 0.0 copy-start.1
  37.7 0.0 copy-start.2
  37.8 13.3 %all-to-all-start.1 = ((bf16[64,8,1024]{2,1,0:T(8,128)(2,1)}), bf16[64,8,1024]{2,1,0:T(8,128)(2,1)S(1)}, u32[]{:S(2)}, u32[]{:S(2)}) async-start(bf16[64,8,1024]{2,1,0:T(8,128)(2,1)} %bitcast.11), calls=%async_computation.1 | async-start | bytes 2097152 | tf_op jit(solution)/shard_map/all_to_all | solution.py:261
  51.1 0.2 shard_map.91
  51.3 3.8 %collective-permute-start.1 = (bf16[2048,128]{1,0:T(8,128)(2,1)S(1)}, bf16[2048,128]{1,0:T(8,128)(2,1)S(1)}, u32[]{:S(2)}, u32[]{:S(2)}) collective-permute-start(bf16[2048,128]{1,0:T(8,128)(2,1)S(1)} %get-tuple-element.36), channel_id=1, source_target_pairs={{0,1},{1,0},{2,3},{3,2},{4,5},{5,4},{6,7},{7,6},{8,9},{9,8},{10,11... | collective-permute-start | bytes 1572872 | tf_op jit(solution)/shard_map/ppermute | solution.py:272
  55.2 2.2 %collective-permute-start.2 = (bf16[2048,128]{1,0:T(8,128)(2,1)S(1)}, bf16[2048,128]{1,0:T(8,128)(2,1)S(1)}, u32[]{:S(2)}, u32[]{:S(2)}) collective-permute-start(bf16[2048,128]{1,0:T(8,128)(2,1)S(1)} %get-tuple-element.37), channel_id=1, source_target_pairs={{0,14},{1,3},{2,0},{3,5},{4,2},{5,7},{6,4},{7,9},{8,6},{9,11},{10,... | collective-permute-start | bytes 1572872 | tf_op jit(solution)/shard_map/ppermute | solution.py:272
  57.4 3.3 %collective-permute-start.3 = (bf16[2048,128]{1,0:T(8,128)(2,1)S(1)}, bf16[2048,128]{1,0:T(8,128)(2,1)S(1)}, u32[]{:S(2)}, u32[]{:S(2)}) collective-permute-start(bf16[2048,128]{1,0:T(8,128)(2,1)S(1)} %get-tuple-element.38), channel_id=1, source_target_pairs={{0,15},{1,2},{2,1},{3,4},{4,3},{5,6},{6,5},{7,8},{8,7},{9,10},{10,... | collective-permute-start | bytes 1572872 | tf_op jit(solution)/shard_map/ppermute | solution.py:272
  60.6 0.0 collective-permute-done.1.refs_0_
  60.7 5.9 %collective-permute-done.2.refs_1_ = bf16[2048,128]{1,0:T(8,128)(2,1)S(1)} collective-permute-done((bf16[2048,128]{1,0:T(8,128)(2,1)S(1)}, bf16[2048,128]{1,0:T(8,128)(2,1)S(1)}, u32[]{:S(2)}, u32[]{:S(2)}) %collective-permute-start.2) | collective-permute-done | bytes 524320 | tf_op jit(solution)/shard_map/ppermute | solution.py:272
  66.6 4.9 %collective-permute-done.3.refs_2_ = bf16[2048,128]{1,0:T(8,128)(2,1)S(1)} collective-permute-done((bf16[2048,128]{1,0:T(8,128)(2,1)S(1)}, bf16[2048,128]{1,0:T(8,128)(2,1)S(1)}, u32[]{:S(2)}, u32[]{:S(2)}) %collective-permute-start.3) | collective-permute-done | bytes 524320 | tf_op jit(solution)/shard_map/ppermute | solution.py:272
  71.5 5.9 %all-to-all-done.1 = bf16[64,8,1024]{2,1,0:T(8,128)(2,1)S(1)} async-done(((bf16[64,8,1024]{2,1,0:T(8,128)(2,1)}), bf16[64,8,1024]{2,1,0:T(8,128)(2,1)S(1)}, u32[]{:S(2)}, u32[]{:S(2)}) %all-to-all-start.1) | async-done | bytes 1048608 | tf_op jit(solution)/shard_map/all_to_all | solution.py:261
  77.4 3.7 %shard_map.92 = bf16[512,512]{1,0:T(8,128)(2,1)} custom-call(s32[1]{0:T(128)} %bitcast.me_ref, bf16[512,1024]{1,0:T(8,128)(2,1)S(1)} %bitcast.7, bf16[4,1024,128]{2,1,0:T(8,128)(2,1)} %up_hbm.3, bf16[4,128,1024]{2,1,0:T(8,128)(2,1)} %down_hbm.3, bf16[2048,128]{1,0:T(8,128)(2,1)S(1)} %collective-permute-done.1.refs_0_, ...), custom_call_target="tpu_custom_call" | custom-call | flops 1073741824 | bytes 9437192 | tf_op jit(solution)/shard_map/pallas_call | solution.py:27
  81.1 9.4 %all-to-all-start.2 = ((bf16[64,8,512]{2,1,0:T(8,128)(2,1)}), bf16[64,8,512]{2,1,0:T(8,128)(2,1)S(1)}, u32[]{:S(2)}, u32[]{:S(2)}) async-start(bf16[64,8,512]{2,1,0:T(8,128)(2,1)} %bitcast.4), calls=%async_computation.2 | async-start | bytes 1048576 | tf_op jit(solution)/shard_map/all_to_all | solution.py:261
  90.6 0.1 shard_map.93
  90.6 3.4 %collective-permute-start.4 = (bf16[512,512]{1,0:T(8,128)(2,1)S(1)}, bf16[512,512]{1,0:T(8,128)(2,1)S(1)}, u32[]{:S(2)}, u32[]{:S(2)}) collective-permute-start(bf16[512,512]{1,0:T(8,128)(2,1)S(1)} %shard_map.93), channel_id=1, source_target_pairs={{0,1},{1,0},{2,3},{3,2},{4,5},{5,4},{6,7},{7,6},{8,9},{9,8},{10,11... | collective-permute-start | bytes 1572872 | tf_op jit(solution)/shard_map/ppermute | solution.py:272
  94.1 1.5 %collective-permute-done.4.got_ref = bf16[512,512]{1,0:T(8,128)(2,1)S(1)} collective-permute-done((bf16[512,512]{1,0:T(8,128)(2,1)S(1)}, bf16[512,512]{1,0:T(8,128)(2,1)S(1)}, u32[]{:S(2)}, u32[]{:S(2)}) %collective-permute-start.4) | collective-permute-done | bytes 524320 | tf_op jit(solution)/shard_map/ppermute | solution.py:272
  95.6 5.6 %shard_map.94 = (bf16[1024,128]{1,0:T(8,128)(2,1)S(1)}, bf16[1024,128]{1,0:T(8,128)(2,1)}, bf16[1024,128]{1,0:T(8,128)(2,1)}, bf16[1024,128]{1,0:T(8,128)(2,1)S(1)}) custom-call(s32[1]{0:T(128)} %bitcast.me_ref, bf16[512,1024]{1,0:T(8,128)(2,1)} %bitcast.9, bf16[512,512]{1,0:T(8,128)(2,1)S(1)} %collective-permute-done.4.got_ref, ...), custom_call_target="tpu_custom_call" | custom-call | flops 1610612736 | bytes 10485768 | tf_op jit(solution)/shard_map/pallas_call | solution.py:27
  101.2 2.3 %collective-permute-start.5 = (bf16[1024,128]{1,0:T(8,128)(2,1)}, bf16[1024,128]{1,0:T(8,128)(2,1)S(1)}, u32[]{:S(2)}, u32[]{:S(2)}) collective-permute-start(bf16[1024,128]{1,0:T(8,128)(2,1)} %get-tuple-element.41), channel_id=1, source_target_pairs={{1,0},{0,1},{3,2},{2,3},{5,4},{4,5},{7,6},{6,7},{9,8},{8,9},{11,10... | collective-permute-start | bytes 786440 | tf_op jit(solution)/shard_map/ppermute | solution.py:272
  103.5 1.9 %collective-permute-start.6 = (bf16[1024,128]{1,0:T(8,128)(2,1)}, bf16[1024,128]{1,0:T(8,128)(2,1)S(1)}, u32[]{:S(2)}, u32[]{:S(2)}) collective-permute-start(bf16[1024,128]{1,0:T(8,128)(2,1)} %get-tuple-element.42), channel_id=1, source_target_pairs={{14,0},{3,1},{0,2},{5,3},{2,4},{7,5},{4,6},{9,7},{6,8},{11,9},{8,1... | collective-permute-start | bytes 786440 | tf_op jit(solution)/shard_map/ppermute | solution.py:272
  105.4 0.1 copy.9.gate_ref
  105.5 0.0 collective-permute-done.5.refs_1_
  105.5 5.6 %collective-permute-done.6.refs_2_ = bf16[1024,128]{1,0:T(8,128)(2,1)S(1)} collective-permute-done((bf16[1024,128]{1,0:T(8,128)(2,1)}, bf16[1024,128]{1,0:T(8,128)(2,1)S(1)}, u32[]{:S(2)}, u32[]{:S(2)}) %collective-permute-start.6) | collective-permute-done | bytes 262176 | tf_op jit(solution)/shard_map/ppermute | solution.py:272
  111.1 0.0 all-to-all-done.2
  111.1 0.3 shard_map.95
  111.5 4.1 %collective-permute-start.7 = (bf16[32,512]{1,0:T(8,128)(2,1)S(1)}, bf16[32,512]{1,0:T(8,128)(2,1)S(1)}, u32[]{:S(2)}, u32[]{:S(2)}) collective-permute-start(bf16[32,512]{1,0:T(8,128)(2,1)S(1)} %get-tuple-element.45), channel_id=1, source_target_pairs={{0,1},{1,0},{2,3},{3,2},{4,5},{5,4},{6,7},{7,6},{8,9},{9,8},{10,11... | collective-permute-start | bytes 98312 | tf_op jit(solution)/shard_map/ppermute | solution.py:272
  115.6 0.8 collective-permute-done.7.got_ref
  116.4 0.7 shard_map.96
  117.2 3.4 %all-to-all-start.3 = ((bf16[8,32,512]{2,1,0:T(8,128)(2,1)}), bf16[8,32,512]{2,1,0:T(8,128)(2,1)S(1)}, u32[]{:S(2)}, u32[]{:S(2)}) async-start(bf16[8,32,512]{2,1,0:T(8,128)(2,1)} %shard_map.96), calls=%async_computation.3 | async-start | bytes 524288 | tf_op jit(solution)/shard_map/all_to_all | solution.py:278
  120.6 3.8 %collective-permute-start.9 = (bf16[1024,128]{1,0:T(8,128)(2,1)S(1)}, bf16[1024,128]{1,0:T(8,128)(2,1)S(1)}, u32[]{:S(2)}, u32[]{:S(2)}) collective-permute-start(bf16[1024,128]{1,0:T(8,128)(2,1)S(1)} %get-tuple-element.49), channel_id=1, source_target_pairs={{15,0},{2,1},{1,2},{4,3},{3,4},{6,5},{5,6},{8,7},{7,8},{10,9},{9,1... | collective-permute-start | bytes 786440 | tf_op jit(solution)/shard_map/ppermute | solution.py:272
  124.4 8.3 %all-to-all-done.3.i_ref = bf16[8,32,512]{2,1,0:T(8,128)(2,1)S(1)} async-done(((bf16[8,32,512]{2,1,0:T(8,128)(2,1)}), bf16[8,32,512]{2,1,0:T(8,128)(2,1)S(1)}, u32[]{:S(2)}, u32[]{:S(2)}) %all-to-all-start.3) | async-done | bytes 262176 | tf_op jit(solution)/shard_map/all_to_all | solution.py:278
  132.7 2.6 %collective-permute-start.8 = (bf16[32,512]{1,0:T(8,128)(2,1)S(1)}, bf16[32,512]{1,0:T(8,128)(2,1)S(1)}, u32[]{:S(2)}, u32[]{:S(2)}) collective-permute-start(bf16[32,512]{1,0:T(8,128)(2,1)S(1)} %shard_map.97.own_ref), channel_id=1, source_target_pairs={{0,1},{1,0},{2,3},{3,2},{4,5},{5,4},{6,7},{7,6},{8,9},{9,8},{10,11... | collective-permute-start | bytes 98312 | tf_op jit(solution)/shard_map/ppermute | solution.py:272
  135.3 0.0 collective-permute-done.9.refs_3_
  135.4 0.0 copy-start.4
  135.4 1.0 shard_map.99
  136.4 0.0 collective-permute-done.8.other_ref
  136.4 0.1 copy-done.4
  136.5 0.8 shard_map.98
  (14 shorter events, 0.1 us)
Async XLA Ops:
  0.6 0.7 copy-start.6
  1.3 1.0 copy-start.3
  2.7 16.9 %collective-permute-start = (bf16[32,512]{1,0:T(8,128)(2,1)S(1)}, bf16[32,512]{1,0:T(8,128)(2,1)S(1)}, u32[]{:S(2)}, u32[]{:S(2)}) collective-permute-start(bf16[32,512]{1,0:T(8,128)(2,1)S(1)} %get-tuple-element.27), channel_id=1, source_target_pairs={{0,1},{1,0},{2,3},{3,2},{4,5},{5,4},{6,7},{7,6},{8,9},{9,8},{10,11... | collective-permute-start | bytes 98312 | tf_op jit(solution)/shard_map/ppermute | solution.py:272
  20.4 3.9 %copy-start.7 = (s32[32,22]{0,1:T(8,128)S(1)}, s32[32,22]{0,1:T(8,128)}, u32[]{:S(2)}) copy-start(s32[32,22]{0,1:T(8,128)} %param.9) | copy-start | bytes 8452
  20.4 3.9 %copy-start.8 = (s32[32,22]{0,1:T(8,128)S(1)}, s32[32,22]{0,1:T(8,128)}, u32[]{:S(2)}) copy-start(s32[32,22]{0,1:T(8,128)} %param.8) | copy-start | bytes 8452
  20.4 15.1 %all-to-all-start = ((bf16[8,32,512]{2,1,0:T(8,128)(2,1)}), bf16[8,32,512]{2,1,0:T(8,128)(2,1)S(1)}, u32[]{:S(2)}, u32[]{:S(2)}) async-start(bf16[8,32,512]{2,1,0:T(8,128)(2,1)} %shard_map.87), calls=%async_computation | async-start | bytes 524288 | tf_op jit(solution)/shard_map/all_to_all | solution.py:278
  35.4 0.8 copy-start.5
  37.7 13.4 %copy-start.1 = (bf16[4,1024,128]{2,1,0:T(8,128)(2,1)S(1)}, bf16[4,1024,128]{2,1,0:T(8,128)(2,1)}, u32[]{:S(2)}) copy-start(bf16[4,1024,128]{2,1,0:T(8,128)(2,1)} %up_hbm.3) | copy-start | bytes 3145732
  37.7 13.4 %copy-start.2 = (bf16[4,128,1024]{2,1,0:T(8,128)(2,1)S(1)}, bf16[4,128,1024]{2,1,0:T(8,128)(2,1)}, u32[]{:S(2)}) copy-start(bf16[4,128,1024]{2,1,0:T(8,128)(2,1)} %down_hbm.3) | copy-start | bytes 3145732
  37.8 39.6 %all-to-all-start.1 = ((bf16[64,8,1024]{2,1,0:T(8,128)(2,1)}), bf16[64,8,1024]{2,1,0:T(8,128)(2,1)S(1)}, u32[]{:S(2)}, u32[]{:S(2)}) async-start(bf16[64,8,1024]{2,1,0:T(8,128)(2,1)} %bitcast.11), calls=%async_computation.1 | async-start | bytes 2097152 | tf_op jit(solution)/shard_map/all_to_all | solution.py:261
  51.3 9.3 %collective-permute-start.1 = (bf16[2048,128]{1,0:T(8,128)(2,1)S(1)}, bf16[2048,128]{1,0:T(8,128)(2,1)S(1)}, u32[]{:S(2)}, u32[]{:S(2)}) collective-permute-start(bf16[2048,128]{1,0:T(8,128)(2,1)S(1)} %get-tuple-element.36), channel_id=1, source_target_pairs={{0,1},{1,0},{2,3},{3,2},{4,5},{5,4},{6,7},{7,6},{8,9},{9,8},{10,11... | collective-permute-start | bytes 1572872 | tf_op jit(solution)/shard_map/ppermute | solution.py:272
  55.2 11.4 %collective-permute-start.2 = (bf16[2048,128]{1,0:T(8,128)(2,1)S(1)}, bf16[2048,128]{1,0:T(8,128)(2,1)S(1)}, u32[]{:S(2)}, u32[]{:S(2)}) collective-permute-start(bf16[2048,128]{1,0:T(8,128)(2,1)S(1)} %get-tuple-element.37), channel_id=1, source_target_pairs={{0,14},{1,3},{2,0},{3,5},{4,2},{5,7},{6,4},{7,9},{8,6},{9,11},{10,... | collective-permute-start | bytes 1572872 | tf_op jit(solution)/shard_map/ppermute | solution.py:272
  57.4 14.1 %collective-permute-start.3 = (bf16[2048,128]{1,0:T(8,128)(2,1)S(1)}, bf16[2048,128]{1,0:T(8,128)(2,1)S(1)}, u32[]{:S(2)}, u32[]{:S(2)}) collective-permute-start(bf16[2048,128]{1,0:T(8,128)(2,1)S(1)} %get-tuple-element.38), channel_id=1, source_target_pairs={{0,15},{1,2},{2,1},{3,4},{4,3},{5,6},{6,5},{7,8},{8,7},{9,10},{10,... | collective-permute-start | bytes 1572872 | tf_op jit(solution)/shard_map/ppermute | solution.py:272
  77.4 13.2 %copy-start = (bf16[64,8,1024]{2,1,0:T(8,128)(2,1)}, bf16[64,8,1024]{2,1,0:T(8,128)(2,1)S(1)}, u32[]{:S(2)}) copy-start(bf16[64,8,1024]{2,1,0:T(8,128)(2,1)S(1)} %all-to-all-done.1) | copy-start | bytes 3145732
  81.1 30.0 %all-to-all-start.2 = ((bf16[64,8,512]{2,1,0:T(8,128)(2,1)}), bf16[64,8,512]{2,1,0:T(8,128)(2,1)S(1)}, u32[]{:S(2)}, u32[]{:S(2)}) async-start(bf16[64,8,512]{2,1,0:T(8,128)(2,1)} %bitcast.4), calls=%async_computation.2 | async-start | bytes 1048576 | tf_op jit(solution)/shard_map/all_to_all | solution.py:261
  90.6 5.0 %collective-permute-start.4 = (bf16[512,512]{1,0:T(8,128)(2,1)S(1)}, bf16[512,512]{1,0:T(8,128)(2,1)S(1)}, u32[]{:S(2)}, u32[]{:S(2)}) collective-permute-start(bf16[512,512]{1,0:T(8,128)(2,1)S(1)} %shard_map.93), channel_id=1, source_target_pairs={{0,1},{1,0},{2,3},{3,2},{4,5},{5,4},{6,7},{7,6},{8,9},{9,8},{10,11... | collective-permute-start | bytes 1572872 | tf_op jit(solution)/shard_map/ppermute | solution.py:272
  101.2 4.3 %collective-permute-start.5 = (bf16[1024,128]{1,0:T(8,128)(2,1)}, bf16[1024,128]{1,0:T(8,128)(2,1)S(1)}, u32[]{:S(2)}, u32[]{:S(2)}) collective-permute-start(bf16[1024,128]{1,0:T(8,128)(2,1)} %get-tuple-element.41), channel_id=1, source_target_pairs={{1,0},{0,1},{3,2},{2,3},{5,4},{4,5},{7,6},{6,7},{9,8},{8,9},{11,10... | collective-permute-start | bytes 786440 | tf_op jit(solution)/shard_map/ppermute | solution.py:272
  103.5 7.6 %collective-permute-start.6 = (bf16[1024,128]{1,0:T(8,128)(2,1)}, bf16[1024,128]{1,0:T(8,128)(2,1)S(1)}, u32[]{:S(2)}, u32[]{:S(2)}) collective-permute-start(bf16[1024,128]{1,0:T(8,128)(2,1)} %get-tuple-element.42), channel_id=1, source_target_pairs={{14,0},{3,1},{0,2},{5,3},{2,4},{7,5},{4,6},{9,7},{6,8},{11,9},{8,1... | collective-permute-start | bytes 786440 | tf_op jit(solution)/shard_map/ppermute | solution.py:272
  111.5 5.0 %collective-permute-start.7 = (bf16[32,512]{1,0:T(8,128)(2,1)S(1)}, bf16[32,512]{1,0:T(8,128)(2,1)S(1)}, u32[]{:S(2)}, u32[]{:S(2)}) collective-permute-start(bf16[32,512]{1,0:T(8,128)(2,1)S(1)} %get-tuple-element.45), channel_id=1, source_target_pairs={{0,1},{1,0},{2,3},{3,2},{4,5},{5,4},{6,7},{7,6},{8,9},{9,8},{10,11... | collective-permute-start | bytes 98312 | tf_op jit(solution)/shard_map/ppermute | solution.py:272
  117.2 15.5 %all-to-all-start.3 = ((bf16[8,32,512]{2,1,0:T(8,128)(2,1)}), bf16[8,32,512]{2,1,0:T(8,128)(2,1)S(1)}, u32[]{:S(2)}, u32[]{:S(2)}) async-start(bf16[8,32,512]{2,1,0:T(8,128)(2,1)} %shard_map.96), calls=%async_computation.3 | async-start | bytes 524288 | tf_op jit(solution)/shard_map/all_to_all | solution.py:278
  120.6 14.8 %collective-permute-start.9 = (bf16[1024,128]{1,0:T(8,128)(2,1)S(1)}, bf16[1024,128]{1,0:T(8,128)(2,1)S(1)}, u32[]{:S(2)}, u32[]{:S(2)}) collective-permute-start(bf16[1024,128]{1,0:T(8,128)(2,1)S(1)} %get-tuple-element.49), channel_id=1, source_target_pairs={{15,0},{2,1},{1,2},{4,3},{3,4},{6,5},{5,6},{8,7},{7,8},{10,9},{9,1... | collective-permute-start | bytes 786440 | tf_op jit(solution)/shard_map/ppermute | solution.py:272
  132.7 3.7 %collective-permute-start.8 = (bf16[32,512]{1,0:T(8,128)(2,1)S(1)}, bf16[32,512]{1,0:T(8,128)(2,1)S(1)}, u32[]{:S(2)}, u32[]{:S(2)}) collective-permute-start(bf16[32,512]{1,0:T(8,128)(2,1)S(1)} %shard_map.97.own_ref), channel_id=1, source_target_pairs={{0,1},{1,0},{2,3},{3,2},{4,5},{5,4},{6,7},{7,6},{8,9},{9,8},{10,11... | collective-permute-start | bytes 98312 | tf_op jit(solution)/shard_map/ppermute | solution.py:272
  135.4 1.2 copy-start.4

commit v2 on v1

--- a/solution.py
+++ b/solution.py
@@ -81,7 +81,8 @@
     o_ref[...] = jnp.sum(i_ref[...].astype(F32), axis=0).astype(BF16)
 
 
-def pick_kernel(me_ref, table_ref, *coef_refs):
+def pick_kernel(me_ref, table_ref, latent_ref, kept_ref, *coef_refs):
+    kept_ref[...] = latent_ref[...]
     count, tokens = coef_refs[0].shape
     top = table_ref.shape[0] // 2
     row = lax.broadcasted_iota(jnp.int32, (count, tokens), 0)
@@ -272,12 +273,13 @@
     return lax.ppermute(array, HEAD, [(b, a) for a, b in pairs] if back else pairs)
 
 
-def sum_over_head(keep, give, beside=()):
+def sum_over_head(keep, give, beside=(), before=()):
     chips = lax.axis_size("z")
-    spread = call(spread_kernel, shape(chips, *keep.shape), keep, swap(give, 1))
+    got, *before = lax.optimization_barrier((swap(give, 1), *before))
+    spread = call(spread_kernel, shape(chips, *keep.shape), keep, got)
     moved = lax.all_to_all(spread, "z", split_axis=0, concat_axis=0, tiled=True)
     moved, *beside = lax.optimization_barrier((moved, *beside))
-    return call(sum_kernel, shape(*keep.shape), moved), *beside
+    return call(sum_kernel, shape(*keep.shape), moved), *beside, *before
 
 
 def per_device(latent, routes, gate_q, up_weight, down_weight, out_weight, cotangent):
@@ -290,7 +292,9 @@
     me = (2 * (lax.axis_index("z") & 1) + lax.axis_index("core")).astype(jnp.int32).reshape(1)
     table = jnp.concatenate([routes, gate_q], axis=1).T
 
-    coefs = call(pick_kernel, [shape(count, tokens)] * 3, me, table, scalars=1)
+    latent, *coefs = call(
+        pick_kernel, [shape(tokens, width)] + [shape(count, tokens)] * 3, me, table, latent, scalars=1
+    )
     packs = call(
         pack_kernel,
         [shape(2 * width, unit)] * (QUAD - 1),
@@ -307,7 +311,7 @@
             pltpu.SemaphoreType.DMA((2,)),
         ],
     )
-    back, table, *coefs = sum_over_head(*back, beside=(table, *coefs))
+    back, table, latent, *coefs = sum_over_head(*back, beside=(table, latent, *coefs))
     send = call(
         send_kernel,
         shape(count, width),
@@ -341,14 +345,14 @@
         scratch=[up_space, down_space, up_space, pltpu.SemaphoreType.DMA((copies + QUAD,))],
     )
     grads = [grads[0]] + [swap(g, d, back=True) for d, g in enumerate(grads[1:], 1)]
-    returned, *grads[1:3] = lax.optimization_barrier((exchange(out, "expert"), *grads[1:3]))
-    grad_up = call(grad_kernel, shape(*up_weight.shape), me, *grads, scalars=1)
+    returned, grads[1] = lax.optimization_barrier((exchange(out, "expert"), grads[1]))
     comb = call(combine_kernel, [half_wide, half], me, returned, coefs[0], gate_q, scalars=1)
-    (comb,) = sum_over_head(*comb)
+    comb, grads[2] = sum_over_head(*comb, before=(grads[2],))
     mixed = call(
         mixed_kernel, shape(tokens, out_weight.shape[1]), me, comb, swap(comb, 1), out_weight,
         scalars=1, flops=2 * tokens * width * out_weight.shape[1],
     )
+    grad_up = call(grad_kernel, shape(*up_weight.shape), me, *grads, scalars=1)
     return (mixed, grad_up)
 
 

time: 138 us -> 135 us (0.978)
  waiting for transfers between devices: 43.6 us -> 39 us
  starting transfers between devices: 73.6 us -> 75.6 us
    ppermute x10, waiting for transfers between devices: 19.6 us -> 14 us  [swap(): lax.ppermute(array, HEAD, [(b, a) for a, b in pairs] if back else pairs)]
    ppermute x10, starting transfers between devices: 43.5 us -> 45.5 us  [swap(): lax.ppermute(array, HEAD, [(b, a) for a, b in pairs] if back else pairs)]
where the time goes in v2:
time: 135 us; the launch traced here: 134 us
  starting transfers between devices  75.6 us (56%)
  waiting for transfers between devices  39 us (29%)
  Pallas kernels  16.5 us (12%)
  local copies, waits for them, and re-layouts  1.99 us (1%)
    ppermute x10, starting transfers between devices, swap(): lax.ppermute(array, HEAD, [(b, a) for a, b in pairs] if back else pairs)  45.5 us
    all_to_all x2, starting transfers between devices, exchange(): moved = lax.all_to_all(split, axis, split_axis=0, concat_axis=0, tiled=True)  22.8 us
    all_to_all x2, waiting for transfers between devices, sum_over_head(): moved = lax.all_to_all(spread, 'z', split_axis=0, concat_axis=0, tiled=True)  18 us
    pallas_call x14, Pallas kernels, call(): pl.pallas_call(kernel, out_shape=outs, in_specs=ins, out_specs=places[0]...  16.5 us
    ppermute x10, waiting for transfers between devices, swap(): lax.ppermute(array, HEAD, [(b, a) for a, b in pairs] if back else pairs)  14 us
    all_to_all x2, starting transfers between devices, sum_over_head(): moved = lax.all_to_all(spread, 'z', split_axis=0, concat_axis=0, tiled=True)  7.3 us
    all_to_all x2, waiting for transfers between devices, exchange(): moved = lax.all_to_all(split, axis, split_axis=0, concat_axis=0, tiled=True)  6.93 us
  transfers between devices with their start and end apart: 14, of which 9 were waited for; matrix products, arithmetic and copies ran while one was open for 0% of the time, Pallas kernels for 6%

profile of v2, /device:TPU:1, one launch (start us, length us, event | category | flops | bytes accessed | tf_op | source)
XLA Modules:
  0.0 134.0 jit_solution(3112625662167354600)
XLA Ops:
  0.6 0.0 copy-start.6
  0.6 0.7 copy-done.6
  1.4 1.0 copy-done.3
  2.4 0.3 shard_map.86
  2.7 16.1 %collective-permute-start = (bf16[32,512]{1,0:T(8,128)(2,1)S(1)}, bf16[32,512]{1,0:T(8,128)(2,1)S(1)}, u32[]{:S(2)}, u32[]{:S(2)}) collective-permute-start(bf16[32,512]{1,0:T(8,128)(2,1)S(1)} %get-tuple-element.30), channel_id=1, source_target_pairs={{0,1},{1,0},{2,3},{3,2},{4,5},{5,4},{6,7},{7,6},{8,9},{9,8},{10,11... | collective-permute-start | bytes 98312 | tf_op jit(solution)/shard_map/ppermute | solution.py:273
  18.8 0.8 collective-permute-done.got_ref
  19.6 0.7 shard_map.87
  20.4 3.9 %all-to-all-start = ((bf16[8,32,512]{2,1,0:T(8,128)(2,1)}), bf16[8,32,512]{2,1,0:T(8,128)(2,1)S(1)}, u32[]{:S(2)}, u32[]{:S(2)}) async-start(bf16[8,32,512]{2,1,0:T(8,128)(2,1)} %shard_map.87), calls=%async_computation | async-start | bytes 524288 | tf_op jit(solution)/shard_map/all_to_all | solution.py:280
  24.3 1.4 %shard_map.88 = (bf16[32,1024]{1,0:T(8,128)(2,1)S(1)}, bf16[512,32]{1,0:T(8,128)(2,1)S(1)}, bf16[512,32]{1,0:T(8,128)(2,1)S(1)}, bf16[512,32]{1,0:T(8,128)(2,1)S(1)}) custom-call(s32[1]{0:T(128)} %bitcast.me_ref, s32[44,32]{1,0:T(8,128)S(1)} %add_bitcast_fusion.table_ref, bf16[32,1024]{1,0:T(8,128)(2,1)S(1)} %copy-done.5), custom_call_target="tpu_custom_call" | custom-call | bytes 142344 | tf_op jit(solution)/shard_map/pallas_call | solution.py:27
  25.7 9.7 %all-to-all-done.i_ref = bf16[8,32,512]{2,1,0:T(8,128)(2,1)S(1)} async-done(((bf16[8,32,512]{2,1,0:T(8,128)(2,1)}), bf16[8,32,512]{2,1,0:T(8,128)(2,1)S(1)}, u32[]{:S(2)}, u32[]{:S(2)}) %all-to-all-start) | async-done | bytes 262176 | tf_op jit(solution)/shard_map/all_to_all | solution.py:280
  35.5 1.4 %shard_map.90 = bf16[512,1024]{1,0:T(8,128)(2,1)} custom-call(s32[44,32]{1,0:T(8,128)S(1)} %add_bitcast_fusion.table_ref, bf16[512,32]{1,0:T(8,128)(2,1)S(1)} %get-tuple-element.36.coef_ref, bf16[512,32]{1,0:T(8,128)(2,1)S(1)} %get-tuple-element.37.coef0_ref, bf16[512,32]{1,0:T(8,128)(2,1)S(1)} %get-tuple-element.38.coef1_ref, ...), custom_call_target="tpu_custom_call" | custom-call | bytes 404480 | tf_op jit(solution)/shard_map/pallas_call | solution.py:27
  36.9 0.0 copy-start.1
  36.9 0.0 copy-start.2
  37.0 13.3 %all-to-all-start.1 = ((bf16[64,8,1024]{2,1,0:T(8,128)(2,1)}), bf16[64,8,1024]{2,1,0:T(8,128)(2,1)S(1)}, u32[]{:S(2)}, u32[]{:S(2)}) async-start(bf16[64,8,1024]{2,1,0:T(8,128)(2,1)} %bitcast.11), calls=%async_computation.1 | async-start | bytes 2097152 | tf_op jit(solution)/shard_map/all_to_all | solution.py:262
  50.3 0.2 shard_map.91
  50.5 3.8 %collective-permute-start.1 = (bf16[2048,128]{1,0:T(8,128)(2,1)S(1)}, bf16[2048,128]{1,0:T(8,128)(2,1)S(1)}, u32[]{:S(2)}, u32[]{:S(2)}) collective-permute-start(bf16[2048,128]{1,0:T(8,128)(2,1)S(1)} %get-tuple-element.41), channel_id=1, source_target_pairs={{0,1},{1,0},{2,3},{3,2},{4,5},{5,4},{6,7},{7,6},{8,9},{9,8},{10,11... | collective-permute-start | bytes 1572872 | tf_op jit(solution)/shard_map/ppermute | solution.py:273
  54.4 2.2 %collective-permute-start.2 = (bf16[2048,128]{1,0:T(8,128)(2,1)S(1)}, bf16[2048,128]{1,0:T(8,128)(2,1)S(1)}, u32[]{:S(2)}, u32[]{:S(2)}) collective-permute-start(bf16[2048,128]{1,0:T(8,128)(2,1)S(1)} %get-tuple-element.42), channel_id=1, source_target_pairs={{0,14},{1,3},{2,0},{3,5},{4,2},{5,7},{6,4},{7,9},{8,6},{9,11},{10,... | collective-permute-start | bytes 1572872 | tf_op jit(solution)/shard_map/ppermute | solution.py:273
  56.6 3.3 %collective-permute-start.3 = (bf16[2048,128]{1,0:T(8,128)(2,1)S(1)}, bf16[2048,128]{1,0:T(8,128)(2,1)S(1)}, u32[]{:S(2)}, u32[]{:S(2)}) collective-permute-start(bf16[2048,128]{1,0:T(8,128)(2,1)S(1)} %get-tuple-element.43), channel_id=1, source_target_pairs={{0,15},{1,2},{2,1},{3,4},{4,3},{5,6},{6,5},{7,8},{8,7},{9,10},{10,... | collective-permute-start | bytes 1572872 | tf_op jit(solution)/shard_map/ppermute | solution.py:273
  59.9 0.0 collective-permute-done.1.refs_0_
  59.9 5.9 %collective-permute-done.2.refs_1_ = bf16[2048,128]{1,0:T(8,128)(2,1)S(1)} collective-permute-done((bf16[2048,128]{1,0:T(8,128)(2,1)S(1)}, bf16[2048,128]{1,0:T(8,128)(2,1)S(1)}, u32[]{:S(2)}, u32[]{:S(2)}) %collective-permute-start.2) | collective-permute-done | bytes 524320 | tf_op jit(solution)/shard_map/ppermute | solution.py:273
  65.8 4.9 %collective-permute-done.3.refs_2_ = bf16[2048,128]{1,0:T(8,128)(2,1)S(1)} collective-permute-done((bf16[2048,128]{1,0:T(8,128)(2,1)S(1)}, bf16[2048,128]{1,0:T(8,128)(2,1)S(1)}, u32[]{:S(2)}, u32[]{:S(2)}) %collective-permute-start.3) | collective-permute-done | bytes 524320 | tf_op jit(solution)/shard_map/ppermute | solution.py:273
  70.7 5.9 %all-to-all-done.1 = bf16[64,8,1024]{2,1,0:T(8,128)(2,1)S(1)} async-done(((bf16[64,8,1024]{2,1,0:T(8,128)(2,1)}), bf16[64,8,1024]{2,1,0:T(8,128)(2,1)S(1)}, u32[]{:S(2)}, u32[]{:S(2)}) %all-to-all-start.1) | async-done | bytes 1048608 | tf_op jit(solution)/shard_map/all_to_all | solution.py:262
  76.6 3.7 %shard_map.92 = bf16[512,512]{1,0:T(8,128)(2,1)} custom-call(s32[1]{0:T(128)} %bitcast.me_ref, bf16[512,1024]{1,0:T(8,128)(2,1)S(1)} %bitcast.7, bf16[4,1024,128]{2,1,0:T(8,128)(2,1)} %up_hbm.3, bf16[4,128,1024]{2,1,0:T(8,128)(2,1)} %down_hbm.3, bf16[2048,128]{1,0:T(8,128)(2,1)S(1)} %collective-permute-done.1.refs_0_, ...), custom_call_target="tpu_custom_call" | custom-call | flops 1073741824 | bytes 9437192 | tf_op jit(solution)/shard_map/pallas_call | solution.py:27
  80.3 9.5 %all-to-all-start.2 = ((bf16[64,8,512]{2,1,0:T(8,128)(2,1)}), bf16[64,8,512]{2,1,0:T(8,128)(2,1)S(1)}, u32[]{:S(2)}, u32[]{:S(2)}) async-start(bf16[64,8,512]{2,1,0:T(8,128)(2,1)} %bitcast.4), calls=%async_computation.2 | async-start | bytes 1048576 | tf_op jit(solution)/shard_map/all_to_all | solution.py:262
  89.8 0.1 shard_map.93
  89.9 3.4 %collective-permute-start.4 = (bf16[512,512]{1,0:T(8,128)(2,1)S(1)}, bf16[512,512]{1,0:T(8,128)(2,1)S(1)}, u32[]{:S(2)}, u32[]{:S(2)}) collective-permute-start(bf16[512,512]{1,0:T(8,128)(2,1)S(1)} %shard_map.93), channel_id=1, source_target_pairs={{0,1},{1,0},{2,3},{3,2},{4,5},{5,4},{6,7},{7,6},{8,9},{9,8},{10,11... | collective-permute-start | bytes 1572872 | tf_op jit(solution)/shard_map/ppermute | solution.py:273
  93.3 1.5 %collective-permute-done.4.got_ref = bf16[512,512]{1,0:T(8,128)(2,1)S(1)} collective-permute-done((bf16[512,512]{1,0:T(8,128)(2,1)S(1)}, bf16[512,512]{1,0:T(8,128)(2,1)S(1)}, u32[]{:S(2)}, u32[]{:S(2)}) %collective-permute-start.4) | collective-permute-done | bytes 524320 | tf_op jit(solution)/shard_map/ppermute | solution.py:273
  94.8 5.6 %shard_map.94 = (bf16[1024,128]{1,0:T(8,128)(2,1)S(1)}, bf16[1024,128]{1,0:T(8,128)(2,1)}, bf16[1024,128]{1,0:T(8,128)(2,1)}, bf16[1024,128]{1,0:T(8,128)(2,1)S(1)}) custom-call(s32[1]{0:T(128)} %bitcast.me_ref, bf16[512,1024]{1,0:T(8,128)(2,1)} %bitcast.9, bf16[512,512]{1,0:T(8,128)(2,1)S(1)} %collective-permute-done.4.got_ref, ...), custom_call_target="tpu_custom_call" | custom-call | flops 1610612736 | bytes 10485768 | tf_op jit(solution)/shard_map/pallas_call | solution.py:27
  100.4 2.3 %collective-permute-start.5 = (bf16[1024,128]{1,0:T(8,128)(2,1)}, bf16[1024,128]{1,0:T(8,128)(2,1)S(1)}, u32[]{:S(2)}, u32[]{:S(2)}) collective-permute-start(bf16[1024,128]{1,0:T(8,128)(2,1)} %get-tuple-element.46), channel_id=1, source_target_pairs={{1,0},{0,1},{3,2},{2,3},{5,4},{4,5},{7,6},{6,7},{9,8},{8,9},{11,10... | collective-permute-start | bytes 786440 | tf_op jit(solution)/shard_map/ppermute | solution.py:273
  102.7 1.9 %collective-permute-start.7 = (bf16[1024,128]{1,0:T(8,128)(2,1)}, bf16[1024,128]{1,0:T(8,128)(2,1)S(1)}, u32[]{:S(2)}, u32[]{:S(2)}) collective-permute-start(bf16[1024,128]{1,0:T(8,128)(2,1)} %get-tuple-element.50), channel_id=1, source_target_pairs={{14,0},{3,1},{0,2},{5,3},{2,4},{7,5},{4,6},{9,7},{6,8},{11,9},{8,1... | collective-permute-start | bytes 786440 | tf_op jit(solution)/shard_map/ppermute | solution.py:273
  104.6 0.1 copy.9.gate_ref
  104.7 0.0 collective-permute-done.5.refs_1_
  104.7 1.0 all-to-all-done.2
  105.8 0.3 shard_map.95
  106.1 6.1 %collective-permute-start.6 = (bf16[32,512]{1,0:T(8,128)(2,1)S(1)}, bf16[32,512]{1,0:T(8,128)(2,1)S(1)}, u32[]{:S(2)}, u32[]{:S(2)}) collective-permute-start(bf16[32,512]{1,0:T(8,128)(2,1)S(1)} %get-tuple-element.49), channel_id=1, source_target_pairs={{0,1},{1,0},{2,3},{3,2},{4,5},{5,4},{6,7},{7,6},{8,9},{9,8},{10,11... | collective-permute-start | bytes 98312 | tf_op jit(solution)/shard_map/ppermute | solution.py:273
  112.2 0.0 collective-permute-done.7.refs_2_
  112.2 0.8 collective-permute-done.6.got_ref
  113.1 0.7 shard_map.96
  113.8 3.4 %all-to-all-start.3 = ((bf16[8,32,512]{2,1,0:T(8,128)(2,1)}), bf16[8,32,512]{2,1,0:T(8,128)(2,1)S(1)}, u32[]{:S(2)}, u32[]{:S(2)}) async-start(bf16[8,32,512]{2,1,0:T(8,128)(2,1)} %shard_map.96), calls=%async_computation.3 | async-start | bytes 524288 | tf_op jit(solution)/shard_map/all_to_all | solution.py:280
  117.2 3.8 %collective-permute-start.9 = (bf16[1024,128]{1,0:T(8,128)(2,1)S(1)}, bf16[1024,128]{1,0:T(8,128)(2,1)S(1)}, u32[]{:S(2)}, u32[]{:S(2)}) collective-permute-start(bf16[1024,128]{1,0:T(8,128)(2,1)S(1)} %get-tuple-element.55), channel_id=1, source_target_pairs={{15,0},{2,1},{1,2},{4,3},{3,4},{6,5},{5,6},{8,7},{7,8},{10,9},{9,1... | collective-permute-start | bytes 786440 | tf_op jit(solution)/shard_map/ppermute | solution.py:273
  121.0 8.3 %all-to-all-done.3.i_ref = bf16[8,32,512]{2,1,0:T(8,128)(2,1)S(1)} async-done(((bf16[8,32,512]{2,1,0:T(8,128)(2,1)}), bf16[8,32,512]{2,1,0:T(8,128)(2,1)S(1)}, u32[]{:S(2)}, u32[]{:S(2)}) %all-to-all-start.3) | async-done | bytes 262176 | tf_op jit(solution)/shard_map/all_to_all | solution.py:280
  129.4 2.6 %collective-permute-start.8 = (bf16[32,512]{1,0:T(8,128)(2,1)S(1)}, bf16[32,512]{1,0:T(8,128)(2,1)S(1)}, u32[]{:S(2)}, u32[]{:S(2)}) collective-permute-start(bf16[32,512]{1,0:T(8,128)(2,1)S(1)} %shard_map.97.own_ref), channel_id=1, source_target_pairs={{0,1},{1,0},{2,3},{3,2},{4,5},{5,4},{6,7},{7,6},{8,9},{9,8},{10,11... | collective-permute-start | bytes 98312 | tf_op jit(solution)/shard_map/ppermute | solution.py:273
  132.0 0.0 collective-permute-done.9.refs_3_
  132.0 0.0 copy-start.4
  132.0 1.0 shard_map.99
  133.0 0.0 collective-permute-done.8.other_ref
  133.1 0.1 copy-done.4
  133.2 0.8 shard_map.98
  (14 shorter events, 0.1 us)
Async XLA Ops:
  0.6 0.7 copy-start.6
  1.3 1.0 copy-start.3
  2.7 16.9 %collective-permute-start = (bf16[32,512]{1,0:T(8,128)(2,1)S(1)}, bf16[32,512]{1,0:T(8,128)(2,1)S(1)}, u32[]{:S(2)}, u32[]{:S(2)}) collective-permute-start(bf16[32,512]{1,0:T(8,128)(2,1)S(1)} %get-tuple-element.30), channel_id=1, source_target_pairs={{0,1},{1,0},{2,3},{3,2},{4,5},{5,4},{6,7},{7,6},{8,9},{9,8},{10,11... | collective-permute-start | bytes 98312 | tf_op jit(solution)/shard_map/ppermute | solution.py:273
  20.4 3.9 %copy-start.7 = (s32[32,22]{0,1:T(8,128)S(1)}, s32[32,22]{0,1:T(8,128)}, u32[]{:S(2)}) copy-start(s32[32,22]{0,1:T(8,128)} %param.9) | copy-start | bytes 8452
  20.4 3.9 %copy-start.8 = (s32[32,22]{0,1:T(8,128)S(1)}, s32[32,22]{0,1:T(8,128)}, u32[]{:S(2)}) copy-start(s32[32,22]{0,1:T(8,128)} %param.8) | copy-start | bytes 8452
  20.4 3.9 %copy-start.5 = (bf16[32,1024]{1,0:T(8,128)(2,1)S(1)}, bf16[32,1024]{1,0:T(8,128)(2,1)}, u32[]{:S(2)}) copy-start(bf16[32,1024]{1,0:T(8,128)(2,1)} %latent_ref.1) | copy-start | bytes 196612
  20.4 15.1 %all-to-all-start = ((bf16[8,32,512]{2,1,0:T(8,128)(2,1)}), bf16[8,32,512]{2,1,0:T(8,128)(2,1)S(1)}, u32[]{:S(2)}, u32[]{:S(2)}) async-start(bf16[8,32,512]{2,1,0:T(8,128)(2,1)} %shard_map.87), calls=%async_computation | async-start | bytes 524288 | tf_op jit(solution)/shard_map/all_to_all | solution.py:280
  36.9 13.4 %copy-start.1 = (bf16[4,1024,128]{2,1,0:T(8,128)(2,1)S(1)}, bf16[4,1024,128]{2,1,0:T(8,128)(2,1)}, u32[]{:S(2)}) copy-start(bf16[4,1024,128]{2,1,0:T(8,128)(2,1)} %up_hbm.3) | copy-start | bytes 3145732
  36.9 13.4 %copy-start.2 = (bf16[4,128,1024]{2,1,0:T(8,128)(2,1)S(1)}, bf16[4,128,1024]{2,1,0:T(8,128)(2,1)}, u32[]{:S(2)}) copy-start(bf16[4,128,1024]{2,1,0:T(8,128)(2,1)} %down_hbm.3) | copy-start | bytes 3145732
  37.0 39.6 %all-to-all-start.1 = ((bf16[64,8,1024]{2,1,0:T(8,128)(2,1)}), bf16[64,8,1024]{2,1,0:T(8,128)(2,1)S(1)}, u32[]{:S(2)}, u32[]{:S(2)}) async-start(bf16[64,8,1024]{2,1,0:T(8,128)(2,1)} %bitcast.11), calls=%async_computation.1 | async-start | bytes 2097152 | tf_op jit(solution)/shard_map/all_to_all | solution.py:262
  50.5 9.3 %collective-permute-start.1 = (bf16[2048,128]{1,0:T(8,128)(2,1)S(1)}, bf16[2048,128]{1,0:T(8,128)(2,1)S(1)}, u32[]{:S(2)}, u32[]{:S(2)}) collective-permute-start(bf16[2048,128]{1,0:T(8,128)(2,1)S(1)} %get-tuple-element.41), channel_id=1, source_target_pairs={{0,1},{1,0},{2,3},{3,2},{4,5},{5,4},{6,7},{7,6},{8,9},{9,8},{10,11... | collective-permute-start | bytes 1572872 | tf_op jit(solution)/shard_map/ppermute | solution.py:273
  54.4 11.4 %collective-permute-start.2 = (bf16[2048,128]{1,0:T(8,128)(2,1)S(1)}, bf16[2048,128]{1,0:T(8,128)(2,1)S(1)}, u32[]{:S(2)}, u32[]{:S(2)}) collective-permute-start(bf16[2048,128]{1,0:T(8,128)(2,1)S(1)} %get-tuple-element.42), channel_id=1, source_target_pairs={{0,14},{1,3},{2,0},{3,5},{4,2},{5,7},{6,4},{7,9},{8,6},{9,11},{10,... | collective-permute-start | bytes 1572872 | tf_op jit(solution)/shard_map/ppermute | solution.py:273
  56.6 14.1 %collective-permute-start.3 = (bf16[2048,128]{1,0:T(8,128)(2,1)S(1)}, bf16[2048,128]{1,0:T(8,128)(2,1)S(1)}, u32[]{:S(2)}, u32[]{:S(2)}) collective-permute-start(bf16[2048,128]{1,0:T(8,128)(2,1)S(1)} %get-tuple-element.43), channel_id=1, source_target_pairs={{0,15},{1,2},{2,1},{3,4},{4,3},{5,6},{6,5},{7,8},{8,7},{9,10},{10,... | collective-permute-start | bytes 1572872 | tf_op jit(solution)/shard_map/ppermute | solution.py:273
  76.6 13.2 %copy-start = (bf16[64,8,1024]{2,1,0:T(8,128)(2,1)}, bf16[64,8,1024]{2,1,0:T(8,128)(2,1)S(1)}, u32[]{:S(2)}) copy-start(bf16[64,8,1024]{2,1,0:T(8,128)(2,1)S(1)} %all-to-all-done.1) | copy-start | bytes 3145732
  80.3 25.4 %all-to-all-start.2 = ((bf16[64,8,512]{2,1,0:T(8,128)(2,1)}), bf16[64,8,512]{2,1,0:T(8,128)(2,1)S(1)}, u32[]{:S(2)}, u32[]{:S(2)}) async-start(bf16[64,8,512]{2,1,0:T(8,128)(2,1)} %bitcast.4), calls=%async_computation.2 | async-start | bytes 1048576 | tf_op jit(solution)/shard_map/all_to_all | solution.py:262
  89.9 4.9 %collective-permute-start.4 = (bf16[512,512]{1,0:T(8,128)(2,1)S(1)}, bf16[512,512]{1,0:T(8,128)(2,1)S(1)}, u32[]{:S(2)}, u32[]{:S(2)}) collective-permute-start(bf16[512,512]{1,0:T(8,128)(2,1)S(1)} %shard_map.93), channel_id=1, source_target_pairs={{0,1},{1,0},{2,3},{3,2},{4,5},{5,4},{6,7},{7,6},{8,9},{9,8},{10,11... | collective-permute-start | bytes 1572872 | tf_op jit(solution)/shard_map/ppermute | solution.py:273
  100.4 4.3 %collective-permute-start.5 = (bf16[1024,128]{1,0:T(8,128)(2,1)}, bf16[1024,128]{1,0:T(8,128)(2,1)S(1)}, u32[]{:S(2)}, u32[]{:S(2)}) collective-permute-start(bf16[1024,128]{1,0:T(8,128)(2,1)} %get-tuple-element.46), channel_id=1, source_target_pairs={{1,0},{0,1},{3,2},{2,3},{5,4},{4,5},{7,6},{6,7},{9,8},{8,9},{11,10... | collective-permute-start | bytes 786440 | tf_op jit(solution)/shard_map/ppermute | solution.py:273
  102.7 9.5 %collective-permute-start.7 = (bf16[1024,128]{1,0:T(8,128)(2,1)}, bf16[1024,128]{1,0:T(8,128)(2,1)S(1)}, u32[]{:S(2)}, u32[]{:S(2)}) collective-permute-start(bf16[1024,128]{1,0:T(8,128)(2,1)} %get-tuple-element.50), channel_id=1, source_target_pairs={{14,0},{3,1},{0,2},{5,3},{2,4},{7,5},{4,6},{9,7},{6,8},{11,9},{8,1... | collective-permute-start | bytes 786440 | tf_op jit(solution)/shard_map/ppermute | solution.py:273
  106.1 7.0 %collective-permute-start.6 = (bf16[32,512]{1,0:T(8,128)(2,1)S(1)}, bf16[32,512]{1,0:T(8,128)(2,1)S(1)}, u32[]{:S(2)}, u32[]{:S(2)}) collective-permute-start(bf16[32,512]{1,0:T(8,128)(2,1)S(1)} %get-tuple-element.49), channel_id=1, source_target_pairs={{0,1},{1,0},{2,3},{3,2},{4,5},{5,4},{6,7},{7,6},{8,9},{9,8},{10,11... | collective-permute-start | bytes 98312 | tf_op jit(solution)/shard_map/ppermute | solution.py:273
  113.8 15.5 %all-to-all-start.3 = ((bf16[8,32,512]{2,1,0:T(8,128)(2,1)}), bf16[8,32,512]{2,1,0:T(8,128)(2,1)S(1)}, u32[]{:S(2)}, u32[]{:S(2)}) async-start(bf16[8,32,512]{2,1,0:T(8,128)(2,1)} %shard_map.96), calls=%async_computation.3 | async-start | bytes 524288 | tf_op jit(solution)/shard_map/all_to_all | solution.py:280
  117.2 14.8 %collective-permute-start.9 = (bf16[1024,128]{1,0:T(8,128)(2,1)S(1)}, bf16[1024,128]{1,0:T(8,128)(2,1)S(1)}, u32[]{:S(2)}, u32[]{:S(2)}) collective-permute-start(bf16[1024,128]{1,0:T(8,128)(2,1)S(1)} %get-tuple-element.55), channel_id=1, source_target_pairs={{15,0},{2,1},{1,2},{4,3},{3,4},{6,5},{5,6},{8,7},{7,8},{10,9},{9,1... | collective-permute-start | bytes 786440 | tf_op jit(solution)/shard_map/ppermute | solution.py:273
  129.4 3.7 %collective-permute-start.8 = (bf16[32,512]{1,0:T(8,128)(2,1)S(1)}, bf16[32,512]{1,0:T(8,128)(2,1)S(1)}, u32[]{:S(2)}, u32[]{:S(2)}) collective-permute-start(bf16[32,512]{1,0:T(8,128)(2,1)S(1)} %shard_map.97.own_ref), channel_id=1, source_target_pairs={{0,1},{1,0},{2,3},{3,2},{4,5},{5,4},{6,7},{7,6},{8,9},{9,8},{10,11... | collective-permute-start | bytes 98312 | tf_op jit(solution)/shard_map/ppermute | solution.py:273
  132.0 1.2 copy-start.4
